TPU v7x, 32 devices: a whole 2x2x4 slice. The times are simulated.
32 devices in a mesh: batch: 8 (over z, x), seq: 4 (over y, core).
Axes of the slice: x: 2, y: 2, z: 4, core: 2. Of those that a mesh axis runs over, the one named last changes fastest.
Arguments:
- hidden_in: bfloat16 [24, 512, 768], P('batch', 'seq'), may hold values from -6 to 6
- cotangent: bfloat16 [24, 512, 768], P('batch', 'seq'), may hold values from -6 to 6
- span_mask: int32 [24, 512], P('batch', 'seq'), may hold values from 0 to 1, as said below
- lengths: int32 [24], P('batch'), may hold values from 128 to 512, as said below
- repeats: int32 [24], P('batch'), may hold values from 1 to 4
- mask_embedding: bfloat16 [768], replicated, may hold values from -6 to 6
- query_weight: bfloat16 [768, 768], replicated, may hold values from -0.21875 to 0.21875
- query_bias: bfloat16 [768], replicated, may hold values from -2 to 2
- key_weight: bfloat16 [768, 768], replicated, may hold values from -0.21875 to 0.21875
- value_weight: bfloat16 [768, 768], replicated, may hold values from -0.21875 to 0.21875
- value_bias: bfloat16 [768], replicated, may hold values from -2 to 2
- output_weight: bfloat16 [768, 768], replicated, may hold values from -2.5 to 2.5
- output_bias: bfloat16 [768], replicated, may hold values from -2 to 2
- mixing_gain: bfloat16 [768], replicated, may hold values from 0.25 to 1.75
- mixing_shift: bfloat16 [768], replicated, may hold values from -2 to 2
- inner_weight: bfloat16 [768, 3072], replicated, may hold values from -0.21875 to 0.21875
- inner_bias: bfloat16 [3072], replicated, may hold values from -2 to 2
- outer_weight: bfloat16 [3072, 768], replicated, may hold values from -0.21875 to 0.21875
- outer_bias: bfloat16 [768], replicated, may hold values from -2 to 2
- final_gain: bfloat16 [768], replicated, may hold values from 0.25 to 1.75
- final_shift: bfloat16 [768], replicated, may hold values from -2 to 2
Outputs:
- layer_out: bfloat16 [24, 512, 768], P('batch', 'seq')
- grad_input: bfloat16 [24, 512, 768], P('batch', 'seq')
- gradient_mask_embedding: float32 [768], replicated
- gradient_query_weight: float32 [768, 768], P('batch', 'seq')
- gradient_query_bias: float32 [768], replicated
- gradient_key_weight: float32 [768, 768], P('batch', 'seq')
- gradient_value_weight: float32 [768, 768], P('batch', 'seq')
- gradient_value_bias: float32 [768], replicated
- gradient_output_weight: float32 [768, 768], P('batch', 'seq')
- gradient_output_bias: float32 [768], replicated
- gradient_mixing_gain: float32 [768], replicated
- gradient_mixing_shift: float32 [768], replicated
- gradient_inner_weight: float32 [768, 3072], P('batch', 'seq')
- gradient_inner_bias: float32 [3072], replicated
- gradient_outer_weight: float32 [3072, 768], P('batch', 'seq')
- gradient_outer_bias: float32 [768], replicated
- gradient_final_gain: float32 [768], replicated
- gradient_final_shift: float32 [768], replicated
Inputs may be any that keep to these rules, and one draw needn't show every extreme that they name: `lengths`: in every aligned block of 3 rows, at least one row has length 512. `span_mask`: A union of runs of 6 positions; each row has a run that ends or starts within two positions of a multiple of 128 without crossing it.
All inputs are finite; a program needn't handle non-finite values.
Results may differ from a plain program's by a relative error of at most 0.015.
Values may be sent and summed in bfloat16 or wider, within the bound.
A program may use at most 128 MiB of HBM per device.

v0:
```python
import jax
import jax.numpy as jnp
from jax import lax
from jax.sharding import PartitionSpec as P

HEADS = 12
HEAD_DIM = 64
WIDEN = 5


def with_halo(x, sides, width):
    for axis, dim in sides:
        count, length = (lax.axis_size(axis), x.shape[dim])
        up = [(i, (i + 1) % count) for i in range(count - 1)]
        down = [(j, i) for i, j in up]
        last = lax.slice_in_dim(x, length - width, length, axis=dim)
        initial = lax.slice_in_dim(x, 0, width, axis=dim)
        before = lax.ppermute(last, axis, up)
        after = lax.ppermute(initial, axis, down)
        x = jnp.concatenate([before, x, after], axis=dim)
    return x


def layer_norm(inputs, gain, shift):
    center = inputs - jnp.mean(inputs, -1, keepdims=True)
    spread = jnp.mean(center * center, -1, keepdims=True)
    return center * lax.rsqrt(spread + 1e-05) * gain + shift


def linear(inputs, weight):
    return jnp.dot(inputs, weight, preferred_element_type=jnp.float32)


def linear_back(grads, weight):
    return lax.dot_general(
        grads, weight, (((1,), (1,)), ((), ())), preferred_element_type=jnp.float32
    )


def contract_rows(left, right):
    return lax.dot_general(
        left, right, (((0,), (0,)), ((), ())), preferred_element_type=jnp.float32
    )


def gelu_exact(inputs):
    return jax.nn.gelu(inputs, approximate=False)


def shards(
    hidden_in,
    cotangent,
    span_mask,
    lengths,
    repeats,
    mask_embedding,
    query_weight,
    query_bias,
    key_weight,
    value_weight,
    value_bias,
    output_weight,
    output_bias,
    mixing_gain,
    mixing_shift,
    inner_weight,
    inner_bias,
    outer_weight,
    outer_bias,
    final_gain,
    final_shift,
):
    rows, stretch, width = hidden_in.shape
    whole = stretch * lax.axis_size("seq")
    scale = HEAD_DIM ** (-0.5)
    offset = lax.axis_index("seq") * stretch
    rim = with_halo(span_mask, (("seq", 1),), WIDEN)
    window = rim[:, 0:stretch]
    for shifted in range(1, 2 * WIDEN + 1):
        window = window + rim[:, shifted : shifted + stretch]
    widened = window > 0
    positions = offset + jnp.arange(stretch, dtype=jnp.int32)
    live = positions[None, :] < lengths[:, None]
    key_live = jnp.arange(whole, dtype=jnp.int32)[None, :] < lengths[:, None]
    masked_in = jnp.where(widened[..., None], mask_embedding[None, None, :], hidden_in)
    flat_in = masked_in.reshape(rows * stretch, width)
    queries = (linear(flat_in, query_weight) + query_bias.astype(jnp.float32)).astype(jnp.bfloat16)
    key_rows = linear(flat_in, key_weight).astype(jnp.bfloat16).reshape(rows, stretch, width)
    value_rows = (linear(flat_in, value_weight) + value_bias.astype(jnp.float32)).astype(
        jnp.bfloat16
    )
    value_rows = value_rows.reshape(rows, stretch, width)
    key_all, value_all = (
        lax.all_gather(key_rows, "seq", axis=1, tiled=True),
        lax.all_gather(value_rows, "seq", axis=1, tiled=True),
    )
    query_heads = queries.reshape(rows, stretch, HEADS, HEAD_DIM)

    def scores_of(key_full):
        key_heads = key_full.reshape(rows, whole, HEADS, HEAD_DIM)
        raw = jnp.einsum(
            "rqhd,rkhd->rhqk", query_heads, key_heads, preferred_element_type=jnp.float32
        )
        return jnp.where(key_live[:, None, None, :], raw * scale, -1e30)

    logits = scores_of(key_all)
    highest = jnp.max(logits, -1, keepdims=True)
    expd = jnp.exp(logits - highest)
    totals = jnp.sum(expd, -1, keepdims=True)
    log_total = highest + jnp.log(totals)
    probs_low = (expd / totals).astype(jnp.bfloat16)
    value_heads = value_all.reshape(rows, whole, HEADS, HEAD_DIM)
    mixed = jnp.einsum(
        "rhqk,rkhd->rqhd", probs_low, value_heads, preferred_element_type=jnp.float32
    )
    mixed = mixed.reshape(rows * stretch, width).astype(jnp.bfloat16)
    attended = linear(mixed, output_weight) + output_bias.astype(jnp.float32)
    residual_one = flat_in.astype(jnp.float32) + attended
    first, norm_back_one = jax.vjp(
        layer_norm, residual_one, mixing_gain.astype(jnp.float32), mixing_shift.astype(jnp.float32)
    )
    first_low = first.astype(jnp.bfloat16)
    inner = linear(first_low, inner_weight) + inner_bias.astype(jnp.float32)
    activated, gelu_back = jax.vjp(gelu_exact, inner)
    activated_low = activated.astype(jnp.bfloat16)
    outer = linear(activated_low, outer_weight) + outer_bias.astype(jnp.float32)
    final, norm_back_two = jax.vjp(
        layer_norm, first + outer, final_gain.astype(jnp.float32), final_shift.astype(jnp.float32)
    )
    layer_out = final.astype(jnp.bfloat16).reshape(rows, stretch, width)
    weighting = repeats.astype(jnp.float32)[:, None] * live.astype(jnp.float32)
    d_final = (cotangent.astype(jnp.float32) * weighting[:, :, None]).reshape(rows * stretch, width)
    d_two, d_final_gain, d_final_shift = norm_back_two(d_final)
    d_outer = d_two.astype(jnp.bfloat16)
    g_outer_weight = contract_rows(activated_low, d_outer)
    g_outer_bias = jnp.sum(d_outer.astype(jnp.float32), 0)
    (d_inner,) = gelu_back(linear_back(d_outer, outer_weight))
    d_inner = d_inner.astype(jnp.bfloat16)
    g_inner_weight = contract_rows(first_low, d_inner)
    g_inner_bias = jnp.sum(d_inner.astype(jnp.float32), 0)
    d_first = linear_back(d_inner, inner_weight) + d_two
    d_one, d_mixing_gain, d_mixing_shift = norm_back_one(d_first)
    d_attended = d_one.astype(jnp.bfloat16)
    g_output_weight = contract_rows(mixed, d_attended)
    g_output_bias = jnp.sum(d_attended.astype(jnp.float32), 0)
    d_mixed = linear_back(d_attended, output_weight).astype(jnp.bfloat16)
    d_mixed_heads = d_mixed.reshape(rows, stretch, HEADS, HEAD_DIM)
    key_back, value_back = (
        lax.all_gather(key_rows, "seq", axis=1, tiled=True),
        lax.all_gather(value_rows, "seq", axis=1, tiled=True),
    )
    probs = jnp.exp(scores_of(key_back) - log_total)
    probs_again = probs.astype(jnp.bfloat16)
    key_heads = key_back.reshape(rows, whole, HEADS, HEAD_DIM)
    value_heads = value_back.reshape(rows, whole, HEADS, HEAD_DIM)
    d_probs = jnp.einsum(
        "rqhd,rkhd->rhqk", d_mixed_heads, value_heads, preferred_element_type=jnp.float32
    )
    centered = d_probs - jnp.sum(probs * d_probs, -1, keepdims=True)
    d_raw = (probs * centered * scale).astype(jnp.bfloat16)
    d_queries = jnp.einsum("rhqk,rkhd->rqhd", d_raw, key_heads, preferred_element_type=jnp.float32)
    d_queries = d_queries.reshape(rows * stretch, width).astype(jnp.bfloat16)
    d_key_part = jnp.einsum(
        "rhqk,rqhd->rkhd", d_raw, query_heads, preferred_element_type=jnp.float32
    )
    d_value_part = jnp.einsum(
        "rhqk,rqhd->rkhd", probs_again, d_mixed_heads, preferred_element_type=jnp.float32
    )
    d_key_sum, d_value_sum = (
        lax.psum_scatter(
            d_key_part.reshape(rows, whole, width), "seq", scatter_dimension=1, tiled=True
        ),
        lax.psum_scatter(
            d_value_part.reshape(rows, whole, width), "seq", scatter_dimension=1, tiled=True
        ),
    )
    d_keys = d_key_sum.astype(jnp.bfloat16).reshape(rows * stretch, width)
    d_values = d_value_sum.astype(jnp.bfloat16).reshape(rows * stretch, width)
    g_query_weight = contract_rows(flat_in, d_queries)
    g_key_weight = contract_rows(flat_in, d_keys)
    g_value_weight = contract_rows(flat_in, d_values)
    g_query_bias = jnp.sum(d_queries.astype(jnp.float32), 0)
    g_value_bias = jnp.sum(d_values.astype(jnp.float32), 0)
    d_input = (
        d_one
        + linear_back(d_queries, query_weight)
        + linear_back(d_keys, key_weight)
        + linear_back(d_values, value_weight)
    ).reshape(rows, stretch, width)
    grad_input = jnp.where(widened[..., None], 0.0, d_input).astype(jnp.bfloat16)
    g_mask = jnp.sum(jnp.where(widened[..., None], d_input, 0.0), (0, 1))
    matrices = (
        g_query_weight,
        g_key_weight,
        g_value_weight,
        g_output_weight,
        g_inner_weight,
        g_outer_weight,
    )
    partial_sums = (
        lax.psum_scatter(matrices[0], "batch", scatter_dimension=0, tiled=True),
        lax.psum_scatter(matrices[1], "batch", scatter_dimension=0, tiled=True),
        lax.psum_scatter(matrices[2], "batch", scatter_dimension=0, tiled=True),
        lax.psum_scatter(matrices[3], "batch", scatter_dimension=0, tiled=True),
        lax.psum_scatter(matrices[4], "batch", scatter_dimension=0, tiled=True),
        lax.psum_scatter(matrices[5], "batch", scatter_dimension=0, tiled=True),
    )
    summed = (
        lax.psum_scatter(partial_sums[0], "seq", scatter_dimension=1, tiled=True),
        lax.psum_scatter(partial_sums[1], "seq", scatter_dimension=1, tiled=True),
        lax.psum_scatter(partial_sums[2], "seq", scatter_dimension=1, tiled=True),
        lax.psum_scatter(partial_sums[3], "seq", scatter_dimension=1, tiled=True),
        lax.psum_scatter(partial_sums[4], "seq", scatter_dimension=1, tiled=True),
        lax.psum_scatter(partial_sums[5], "seq", scatter_dimension=1, tiled=True),
    )
    vectors = lax.psum(
        (
            g_mask,
            g_query_bias,
            g_value_bias,
            g_output_bias,
            d_mixing_gain,
            d_mixing_shift,
            g_inner_bias,
            g_outer_bias,
            d_final_gain,
            d_final_shift,
        ),
        ("batch", "seq"),
    )
    return (
        layer_out,
        grad_input,
        vectors[0],
        summed[0],
        vectors[1],
        summed[1],
        summed[2],
        vectors[2],
        summed[3],
        vectors[3],
        vectors[4],
        vectors[5],
        summed[4],
        vectors[6],
        summed[5],
        vectors[7],
        vectors[8],
        vectors[9],
    )


def solution(mesh):
    return jax.shard_map(
        shards,
        mesh=mesh,
        in_specs=(
            P("batch", "seq", None),
            P("batch", "seq", None),
            P("batch", "seq"),
            P("batch"),
            P("batch"),
            P(),
            P(),
            P(),
            P(),
            P(),
            P(),
            P(),
            P(),
            P(),
            P(),
            P(),
            P(),
            P(),
            P(),
            P(),
            P(),
        ),
        out_specs=(
            P("batch", "seq", None),
            P("batch", "seq", None),
            P(),
            P("batch", "seq"),
            P(),
            P("batch", "seq"),
            P("batch", "seq"),
            P(),
            P("batch", "seq"),
            P(),
            P(),
            P(),
            P("batch", "seq"),
            P(),
            P("batch", "seq"),
            P(),
            P(),
            P(),
        ),
        check_vma=False,
    )
```

profile of v0, /device:TPU:0, one launch (start us, length us, event | category | flops | bytes accessed | tf_op | source)
XLA Modules:
  0.0 1015.1 jit_solution(12412811156414102943)
XLA Ops:
  33.5 14.0 %all-gather.5.cloned.1.call-done = bf16[3,512,768]{2,1,0:T(8,128)(2,1)} async-done(((bf16[3,128,768]{2,1,0:T(8,128)(2,1)}), bf16[3,512,768]{2,1,0:T(8,128)(2,1)}) %all-gather.5.cloned.1.call-update) | async-done | bytes 2359312 | tf_op jit(solution)/shard_map/all_gather | solution.py:94
  59.6 14.1 %all-gather.3.cloned.1.call-done = bf16[3,512,768]{2,1,0:T(8,128)(2,1)} async-done(((bf16[3,128,768]{2,1,0:T(8,128)(2,1)}), bf16[3,512,768]{2,1,0:T(8,128)(2,1)}) %all-gather.3.cloned.1.call-update) | async-done | bytes 2359312 | tf_op jit(solution)/shard_map/all_gather | solution.py:95
  78.1 6.1 fusion.34
  85.9 14.0 %multiply_convert_fusion.1 = (bf16[384,3072]{1,0:T(8,128)(2,1)S(1)}, f32[384,3072]{1,0:T(8,128)S(1)}, f32[384,3072]{1,0:T(8,128)}) fusion(f32[3072]{0:T(1024)S(1)} %copy-done.27, bf16[768,3072]{1,0:T(8,128)(2,1)S(1)} %bitcast.136, f32[384,768]{1,0:T(8,128)S(1)} %get-tuple-element.109, f32[768]{0:T(1024)S(1)} %convert_element_type.135, ...), kind=kOutput, calls=%fused_computation.18 | convolution fusion | flops 1891270656 | bytes 17716224 | tf_op jit(solution)/shard_map/dot_general | solution.py:31
  105.6 6.1 convert_reduce_fusion
  124.1 8.4 fusion.13
  132.5 6.1 copy.76
  139.2 7.9 fusion.90
  147.0 37.8 %fusion.7 = f32[3,12,64,512]{3,2,1,0:T(8,128)} fusion(bf16[3,128,12,64]{1,3,2,0:T(8,128)(2,1)} %copy-done.13, f32[3,12,128,512]{3,2,1,0:T(8,128)} %fusion.90, f32[3,12,128,512]{3,2,1,0:T(8,128)} %copy-done.1, f32[3,12,128]{2,1,0:T(8,128)} %log_add_fusion, pred[3,512]{1,0:T(4,128)(4,1)S(1)} %iota_compare_fusion), kind=kOutput, calls=%fused_computation.11 | convolution fusion | flops 327947264 | bytes 24202752 | tf_op jit(solution)/shard_map/rhqk,rqhd->rkhd/dot_general | solution.py:163
  184.8 6.0 copy.74
  194.8 37.9 %convert_reduce_fusion.4 = (f32[12,64]{1,0:T(8,128)}, bf16[3,128,12,64]{1,3,2,0:T(8,128)(2,1)}) fusion(bf16[3,512,12,64]{1,3,2,0:T(8,128)(2,1)} %bitcast.109, f32[3,12,128,512]{3,2,1,0:T(8,128)} %fusion.90, f32[3,12,128]{2,1,0:T(8,128)} %log_add_fusion, f32[3,12,128,512]{3,2,1,0:T(8,128)} %copy-done.1, pred[3,512]{1,0:T(4,128)(4,1)S(1)} %iota_compare_fusion), kind=kOutput, calls=%fused_computation.65 | convolution fusion | flops 328831232 | bytes 21846528 | tf_op jit(solution)/shard_map/rhqk,rkhd->rqhd/dot_general | solution.py:161
  250.3 7.0 fusion.79
  258.3 8.0 fusion.91
  266.4 44.8 %reduce-scatter.35.cloned.1.call-done = f32[96,768]{1,0:T(8,128)} async-done(((f32[768,768]{1,0:T(8,128)}), f32[96,768]{1,0:T(8,128)}) %reduce-scatter.35.cloned.1.call-update) | async-done | bytes 294928 | tf_op jit(solution)/shard_map/reduce_scatter | solution.py:204
  313.1 69.7 %reduce-scatter.29.cloned.1.call-done = f32[96,768]{1,0:T(8,128)} async-done(((f32[768,768]{1,0:T(8,128)}), f32[96,768]{1,0:T(8,128)}) %reduce-scatter.29.cloned.1.call-update) | async-done | bytes 294928 | tf_op jit(solution)/shard_map/reduce_scatter | solution.py:201
  385.0 69.5 %reduce-scatter.33.cloned.1.call-done = f32[96,768]{1,0:T(8,128)} async-done(((f32[768,768]{1,0:T(8,128)}), f32[96,768]{1,0:T(8,128)}) %reduce-scatter.33.cloned.1.call-update) | async-done | bytes 294928 | tf_op jit(solution)/shard_map/reduce_scatter | solution.py:203
  456.4 69.7 %reduce-scatter.31.cloned.1.call-done = f32[96,768]{1,0:T(8,128)} async-done(((f32[768,768]{1,0:T(8,128)}), f32[96,768]{1,0:T(8,128)}) %reduce-scatter.31.cloned.1.call-update) | async-done | bytes 294928 | tf_op jit(solution)/shard_map/reduce_scatter | solution.py:202
  528.0 164.2 %reduce-scatter.37.cloned.1.call-done = f32[96,3072]{1,0:T(8,128)} async-done(((f32[768,3072]{1,0:T(8,128)}), f32[96,3072]{1,0:T(8,128)}) %reduce-scatter.37.cloned.1.call-update) | async-done | bytes 1179664 | tf_op jit(solution)/shard_map/reduce_scatter | solution.py:205
  692.2 166.0 %reduce-scatter.41.cloned.1.call-done = f32[384,768]{1,0:T(8,128)} async-done(((f32[3072,768]{1,0:T(8,128)}), f32[384,768]{1,0:T(8,128)}) %reduce-scatter.41.cloned.1.call-update) | async-done | bytes 1179664 | tf_op jit(solution)/shard_map/reduce_scatter | solution.py:206
  864.8 15.9 %reduce-scatter.49.cloned.1.call-done = f32[192,96]{1,0:T(8,128)} async-done(((f32[768,96]{1,0:T(8,128)}), f32[192,96]{1,0:T(8,128)}) %reduce-scatter.49.cloned.1.call-update) | async-done | bytes 73744
  882.3 21.6 %reduce-scatter.43.cloned.1.call-done = f32[192,96]{1,0:T(8,128)} async-done(((f32[768,96]{1,0:T(8,128)}), f32[192,96]{1,0:T(8,128)}) %reduce-scatter.43.cloned.1.call-update) | async-done | bytes 73744
  909.7 41.1 %all-reduce = (f32[768]{0:T(1024)}, f32[768]{0:T(1024)}, f32[768]{0:T(1024)}, f32[768]{0:T(1024)}, f32[768]{0:T(1024)}, /*index=5*/f32[768]{0:T(1024)}, f32[3072...) all-reduce(f32[768]{0:T(1024)} %get-tuple-element.114, ...), channel_id=1, replica_groups=mesh['batch'=8,'seq'=4] {'batch','seq'}, use_global_device_ids=true, to_apply=%region_14.15 | all-reduce | flops 9984 | bytes 79872 | tf_op jit(solution)/shard_map/psum | solution.py:216
  955.7 23.6 %reduce-scatter.39.cloned.1.call-done = f32[96,768]{1,0:T(8,128)} async-done(((f32[96,3072]{1,0:T(8,128)}), f32[96,768]{1,0:T(8,128)}) %reduce-scatter.39.cloned.1.call-update) | async-done | bytes 294928 | tf_op jit(solution)/shard_map/reduce_scatter | solution.py:213
  979.4 28.9 %reduce-scatter.51.cloned.1.call-done = f32[192,384]{1,0:T(8,128)} async-done(((f32[768,384]{1,0:T(8,128)}), f32[192,384]{1,0:T(8,128)}) %reduce-scatter.51.cloned.1.call-update) | async-done | bytes 294928
  (206 shorter events, 112.0 us)
Async XLA Ops:
  7.3 40.1 %all-gather.5.cloned.1.call-start = ((), (), s32[]{:S(2)}) async-start(), calls=%async_computation.15 | async-start | bytes 2949120 | tf_op jit(solution)/shard_map/all_gather | solution.py:94
  8.2 7.5 collective-permute-start
  10.6 5.2 collective-permute-start.1
  20.9 52.8 %all-gather.3.cloned.1.call-start = ((), (), s32[]{:S(2)}) async-start(), calls=%async_computation.14 | async-start | bytes 2949120 | tf_op jit(solution)/shard_map/all_gather | solution.py:95
  23.1 215.4 %reduce-scatter.27.cloned.1.call-start = ((), (), s32[]{:S(2)}) async-start(), calls=%async_computation.17 | async-start | bytes 5898240 | tf_op jit(solution)/shard_map/reduce_scatter | solution.py:173
  138.7 106.1 %reduce-scatter.25.cloned.1.call-start = ((), (), s32[]{:S(2)}) async-start(), calls=%async_computation.16 | async-start | bytes 5898240 | tf_op jit(solution)/shard_map/reduce_scatter | solution.py:170
  190.9 120.2 %reduce-scatter.35.cloned.1.call-start = ((), (), s32[]{:S(2)}) async-start(), calls=%async_computation.21 | async-start | bytes 2654208 | tf_op jit(solution)/shard_map/reduce_scatter | solution.py:204
  194.6 188.2 %reduce-scatter.29.cloned.1.call-start = ((), (), s32[]{:S(2)}) async-start(), calls=%async_computation.18 | async-start | bytes 2654208 | tf_op jit(solution)/shard_map/reduce_scatter | solution.py:201
  238.5 216.0 %reduce-scatter.33.cloned.1.call-start = ((), (), s32[]{:S(2)}) async-start(), calls=%async_computation.20 | async-start | bytes 2654208 | tf_op jit(solution)/shard_map/reduce_scatter | solution.py:203
  244.7 281.3 %reduce-scatter.31.cloned.1.call-start = ((), (), s32[]{:S(2)}) async-start(), calls=%async_computation.19 | async-start | bytes 2654208 | tf_op jit(solution)/shard_map/reduce_scatter | solution.py:202
  250.2 442.0 %reduce-scatter.37.cloned.1.call-start = ((), (), s32[]{:S(2)}) async-start(), calls=%async_computation.22 | async-start | bytes 10616832 | tf_op jit(solution)/shard_map/reduce_scatter | solution.py:205
  257.2 600.9 %reduce-scatter.41.cloned.1.call-start = ((), (), s32[]{:S(2)}) async-start(), calls=%async_computation.24 | async-start | bytes 10616832 | tf_op jit(solution)/shard_map/reduce_scatter | solution.py:206
  266.3 594.6 %copy-start.28 = (f32[12,64]{1,0:T(8,128)S(1)}, f32[12,64]{1,0:T(8,128)}, u32[]{:S(2)}) copy-start(f32[12,64]{1,0:T(8,128)} %get-tuple-element.116) | copy-start | bytes 9220
  266.3 595.2 %copy-start.21 = (f32[384]{0:T(512)S(1)}, f32[384]{0:T(512)}, u32[]{:S(2)}) copy-start(f32[384]{0:T(512)} %copy-done.20) | copy-start | bytes 4612
  266.3 614.3 %reduce-scatter.49.cloned.1.call-start = ((), (), s32[]{:S(2)}) async-start(), calls=%async_computation.28 | async-start | bytes 491520
  313.1 590.8 %reduce-scatter.43.cloned.1.call-start = ((), (), s32[]{:S(2)}) async-start(), calls=%async_computation.25 | async-start | bytes 491520
  384.7 567.8 %reduce-scatter.47.cloned.1.call-start = ((), (), s32[]{:S(2)}) async-start(), calls=%async_computation.27 | async-start | bytes 491520
  456.3 497.8 %reduce-scatter.45.cloned.1.call-start = ((), (), s32[]{:S(2)}) async-start(), calls=%async_computation.26 | async-start | bytes 491520
  527.9 377.5 %copy-start.5 = (bf16[3,128,768]{2,1,0:T(8,128)(2,1)S(1)}, bf16[3,128,768]{2,1,0:T(8,128)(2,1)}, u32[]{:S(2)}) copy-start(bf16[3,128,768]{2,1,0:T(8,128)(2,1)} %copy-done.4) | copy-start | bytes 1769476
  528.0 451.4 %reduce-scatter.39.cloned.1.call-start = ((), (), s32[]{:S(2)}) async-start(), calls=%async_computation.23 | async-start | bytes 1474560 | tf_op jit(solution)/shard_map/reduce_scatter | solution.py:213
  692.2 316.1 %reduce-scatter.51.cloned.1.call-start = ((), (), s32[]{:S(2)}) async-start(), calls=%async_computation.29 | async-start | bytes 1474560
  860.9 46.9 %copy-start.10 = (bf16[3,128,768]{2,1,0:T(8,128)(2,1)S(1)}, bf16[3,128,768]{2,1,0:T(8,128)(2,1)}, u32[]{:S(2)}) copy-start(bf16[3,128,768]{2,1,0:T(8,128)(2,1)} %copy-done.9) | copy-start | bytes 1769476
  864.8 45.0 %copy-start.24 = (f32[768]{0:T(1024)S(1)}, f32[768]{0:T(1024)}, u32[]{:S(2)}) copy-start(f32[768]{0:T(1024)} %get-tuple-element.87) | copy-start | bytes 9220
  864.8 45.0 %copy-start.25 = (f32[768]{0:T(1024)S(1)}, f32[768]{0:T(1024)}, u32[]{:S(2)}) copy-start(f32[768]{0:T(1024)} %get-tuple-element.91) | copy-start | bytes 9220
  (40 other events, 471.5 us)
Sparse Core Ops, SparseCore 0:
  21.1 26.3 all-gather.4
  49.6 24.0 all-gather.2
  138.8 47.9 reduce-scatter.26
  191.0 47.6 reduce-scatter.24
  242.1 69.0 reduce-scatter.34
  314.5 68.2 reduce-scatter.28
  386.3 68.0 reduce-scatter.32
  457.9 68.0 reduce-scatter.30
  529.6 162.4 reduce-scatter.36
  695.6 162.5 reduce-scatter.40
  860.7 19.9 reduce-scatter.48
  883.0 20.7 reduce-scatter.42
  906.4 20.8 reduce-scatter.46
  929.6 21.2 reduce-scatter.44
  954.0 25.3 reduce-scatter.38
  982.5 25.7 reduce-scatter.50
where the time goes:
time: 1020 us
  waiting for transfers between devices  705 us (69%)
  matrix products  171 us (17%)
  local copies, waits for them, and re-layouts  58 us (6%)
  blocking collectives  41.1 us (4%)
  other arithmetic  19.6 us (2%)
  between operations  14.8 us (1%)
    reduce_scatter x1, waiting for transfers between devices, shards(): lax.psum_scatter(matrices[5], 'batch', scatter_dimension=0, tiled=True)  166 us
    reduce_scatter x1, waiting for transfers between devices, shards(): lax.psum_scatter(matrices[4], 'batch', scatter_dimension=0, tiled=True)  164 us
    reduce_scatter x1, waiting for transfers between devices, shards(): lax.psum_scatter(matrices[0], 'batch', scatter_dimension=0, tiled=True)  69.7 us
    reduce_scatter x1, waiting for transfers between devices, shards(): lax.psum_scatter(matrices[1], 'batch', scatter_dimension=0, tiled=True)  69.7 us
    reduce_scatter x1, waiting for transfers between devices, shards(): lax.psum_scatter(matrices[2], 'batch', scatter_dimension=0, tiled=True)  69.5 us
    unnamed x21, waiting for transfers between devices  66.6 us
    reduce_scatter x1, waiting for transfers between devices, shards(): lax.psum_scatter(matrices[3], 'batch', scatter_dimension=0, tiled=True)  44.8 us
    psum x1, blocking collectives, shards(): lax.psum((g_mask, g_query_bias, g_value_bias, g_output_bias, d_mixing_gai...  41.1 us
  transfers between devices with their start and end apart: 18, of which 13 were waited for; matrix products, arithmetic and copies ran while one was open for 17% of the time, Pallas kernels for 0%

commit v1 on v0

--- a/solution.py
+++ b/solution.py
@@ -1,6 +1,10 @@
+import functools
+
 import jax
 import jax.numpy as jnp
 from jax import lax
+from jax.experimental import pallas as pl
+from jax.experimental.pallas import tpu as pltpu
 from jax.sharding import PartitionSpec as P
 
 HEADS = 12
@@ -45,6 +49,255 @@
 
 def gelu_exact(inputs):
     return jax.nn.gelu(inputs, approximate=False)
+
+
+MESH = pl.DeviceIdType.MESH
+PHASES = 5
+
+
+def places():
+    b, s = lax.axis_index("batch"), lax.axis_index("seq")
+    x, zlo, zhi = lax.rem(b, 2), lax.rem(b // 2, 2), b // 4
+    core, y = lax.rem(s, 2), s // 2
+    spot = {"core": core, "x": x, "y": y, "zlo": zlo, "zhi": zhi}
+    peer = {
+        "core": (b, s + 1 - 2 * core),
+        "y": (b, s + 2 - 4 * y),
+        "x": (b + 1 - 2 * x, s),
+        "zlo": (b + 2 - 4 * zlo, s),
+        "zhi": (b + 4 - 8 * zhi, s),
+    }
+    return spot, peer
+
+
+def each_block(shape, body):
+    count = 1
+    for size in shape:
+        count *= size
+
+    def step(n, carry):
+        place = []
+        for size in reversed(shape):
+            place.append(lax.rem(n, size))
+            n = n // size
+        body(tuple(reversed(place)))
+        return carry
+
+    lax.fori_loop(0, count, step, 0)
+
+
+class Unit:
+    def __init__(self, number, order, own, inbox, sends, recvs, spot, peer):
+        self.number, self.order, self.own, self.inbox = number, order, own, inbox
+        self.sends, self.recvs, self.spot, self.peer = sends, recvs, spot, peer
+
+    def axis(self, phase):
+        return ("core", *self.order, "zlo", "zhi")[phase]
+
+    def where(self, phase, stays):
+        spot = self.spot
+        first = self.order[0]
+        here = lambda name: spot[name] if stays else 1 - spot[name]
+        if phase == 1 and first == "x":
+            return (slice(None), slice(None), slice(None), here("x"))
+        if phase == 1:
+            return (here("y"),)
+        if phase == 2 and first == "x":
+            return (here("y"), slice(None), slice(None), spot["x"])
+        if phase == 2:
+            return (spot["y"], slice(None), slice(None), here("x"))
+        if phase == 3:
+            return (spot["y"], slice(None), here("zlo"), spot["x"])
+        return (spot["y"], here("zhi"), spot["zlo"], spot["x"])
+
+    def copy(self, phase):
+        return pltpu.make_async_remote_copy(
+            src_ref=self.own.at[self.where(phase, False)],
+            dst_ref=self.inbox[phase],
+            send_sem=self.sends.at[self.number, phase],
+            recv_sem=self.recvs.at[self.number, phase],
+            device_id=self.peer[self.axis(phase)],
+            device_id_type=MESH,
+        )
+
+    def start(self, phase):
+        self.copy(phase).start()
+
+    def add(self, phase):
+        came = self.inbox[phase]
+        if phase == 0:
+            target = self.own
+        else:
+            target = self.own.at[self.where(phase, True)]
+        lead = came.shape[:-2]
+
+        def body(place):
+            target[place] = target[place] + came[place]
+
+        if lead:
+            each_block(lead, body)
+        else:
+            target[...] = target[...] + came[...]
+
+
+GRAINS = ((192, 384), (96, 768), (48, 384), (48, 384), (48, 384), (48, 384))
+ORDERS = (("x", "y"), ("y", "x"), ("x", "y"), ("y", "x"), ("x", "y"), ("y", "x"))
+
+
+def inbox_shapes(order, grain):
+    return (
+        (2, 2, 2, 2) + grain,
+        ((2, 2, 2) if order[0] == "x" else (2, 2, 2)) + grain,
+        (2, 2) + grain,
+        (2,) + grain,
+        grain,
+        grain,
+    )
+
+
+def reduce_body(*refs):
+    mats, vec_in = refs[:6], refs[6]
+    outs, vec_out = refs[7:13], refs[13]
+    rest = list(refs[14:])
+    owns = [rest.pop(0) for _ in range(6)]
+    inboxes = [[rest.pop(0) for _ in range(6)] for _ in range(6)]
+    final = [rest.pop(0) for _ in range(6)]
+    vec, vec_came = rest.pop(0), rest.pop(0)
+    sends, recvs, local = rest
+    spot, peer = places()
+    core = spot["core"]
+    names = ("core", "x", "y", "zlo", "zhi")
+    barrier = pltpu.get_barrier_semaphore()
+    for name in names:
+        pl.semaphore_signal(barrier, inc=1, device_id=peer[name], device_id_type=MESH)
+    pl.semaphore_wait(barrier, len(names))
+
+    def piece(u, y, side):
+        if u == 1:
+            start = pl.multiple_of((2 * y + side) * 768, 128)
+            return mats[u].at[:, :, :, :, pl.ds(start, 768)]
+        return mats[u].at[:, :, :, side, :, pl.ds(y * 384, 384)]
+
+    first_sends, first_locals = [], []
+    for u in range(6):
+        for y in range(2):
+            go = pltpu.make_async_remote_copy(
+                src_ref=piece(u, y, 1 - core),
+                dst_ref=inboxes[u][0].at[y],
+                send_sem=sends.at[u, 6 + y],
+                recv_sem=recvs.at[u, 6 + y],
+                device_id=peer["core"],
+                device_id_type=MESH,
+            )
+            go.start()
+            keep = pltpu.make_async_copy(piece(u, y, core), owns[u].at[y], local.at[u, y])
+            keep.start()
+            first_sends.append(go)
+            first_locals.append(keep)
+    units = [
+        Unit(u, ORDERS[u], owns[u], inboxes[u], sends, recvs, spot, peer) for u in range(6)
+    ]
+
+    def vector_copy(phase):
+        return pltpu.make_async_remote_copy(
+            src_ref=vec.at[phase],
+            dst_ref=vec_came.at[phase],
+            send_sem=sends.at[6, phase],
+            recv_sem=recvs.at[6, phase],
+            device_id=peer[names[phase]],
+            device_id_type=MESH,
+        )
+
+    vec[0] = vec_in[...]
+    vector_copy(0).start()
+    for phase in range(PHASES):
+        for u, unit in enumerate(units):
+            if phase == 0:
+                for y in range(2):
+                    first_sends[2 * u + y].wait()
+                    first_locals[2 * u + y].wait()
+            else:
+                unit.copy(phase).wait()
+            if phase < 4:
+                unit.add(phase)
+                unit.start(phase + 1)
+        vector_copy(phase).wait()
+        vec[phase + 1] = vec[phase] + vec_came[phase]
+        if phase < 4:
+            vector_copy(phase + 1).start()
+    vec_out[...] = vec[5]
+    swaps = []
+    for u, unit in enumerate(units):
+        mine = (spot["y"], spot["zhi"], spot["zlo"], spot["x"])
+        total = owns[u][mine].astype(jnp.float32) + inboxes[u][4][...].astype(jnp.float32)
+        if u == 1:
+            outs[u][...] = total
+            continue
+        final[u][...] = total.astype(jnp.bfloat16)
+        swap = pltpu.make_async_remote_copy(
+            src_ref=final[u],
+            dst_ref=inboxes[u][5],
+            send_sem=sends.at[u, 5],
+            recv_sem=recvs.at[u, 5],
+            device_id=peer["core"],
+            device_id_type=MESH,
+        )
+        swap.start()
+        swaps.append((u, swap, total))
+    for u, swap, total in swaps:
+        rows = total.shape[0]
+        swap.wait()
+        pick = lambda v: jnp.where(core == 0, v[:, :192], pltpu.roll(v, 192, 1)[:, :192])
+        outs[u][pl.ds(core * rows, rows), :] = pick(total)
+        outs[u][pl.ds((1 - core) * rows, rows), :] = pick(inboxes[u][5][...].astype(jnp.float32))
+
+
+def reduce_plain(mats, vectors):
+    summed = []
+    for mat in mats:
+        part = lax.psum_scatter(
+            mat.astype(jnp.float32), "seq", scatter_dimension=1, tiled=True
+        )
+        summed.append(lax.psum_scatter(part, "batch", scatter_dimension=0, tiled=True))
+    return summed, lax.psum(vectors, ("batch", "seq"))
+
+
+def reduce_gradients(mats, vectors):
+    if lax.axis_size("batch") != 8 or lax.axis_size("seq") != 4:
+        return reduce_plain(mats, vectors)
+    split = []
+    for u, mat in enumerate(mats):
+        rows, cols = GRAINS[u]
+        lead = (2, 2, 2) if u == 1 else (2, 2, 2, 2)
+        split.append(mat.reshape(lead + (rows, mat.shape[1])))
+    outs = [jax.ShapeDtypeStruct((2 * r, 192), jnp.float32) for r, _ in GRAINS]
+    outs[1] = jax.ShapeDtypeStruct((96, 768), jnp.float32)
+    outs.append(jax.ShapeDtypeStruct(vectors.shape, jnp.float32))
+    bf = lambda shape: pltpu.VMEM(shape, jnp.bfloat16)
+    scratch = [bf((2, 2, 2, 2) + grain) for grain in GRAINS]
+    for order, grain in zip(ORDERS, GRAINS):
+        scratch += [bf(shape) for shape in inbox_shapes(order, grain)]
+    scratch += [bf(grain) for grain in GRAINS]
+    scratch += [
+        pltpu.VMEM((6,) + vectors.shape, jnp.float32),
+        pltpu.VMEM((5,) + vectors.shape, jnp.float32),
+        pltpu.SemaphoreType.DMA((7, 8)),
+        pltpu.SemaphoreType.DMA((7, 8)),
+        pltpu.SemaphoreType.DMA((6, 2)),
+    ]
+    vmem = pl.BlockSpec(memory_space=pltpu.VMEM)
+    result = pl.pallas_call(
+        reduce_body,
+        out_shape=outs,
+        in_specs=[pl.BlockSpec(memory_space=pl.ANY)] * 6 + [vmem],
+        out_specs=[vmem] * 7,
+        scratch_shapes=scratch,
+        compiler_params=pltpu.CompilerParams(
+            collective_id=1, has_side_effects=True, vmem_limit_bytes=56 * 2**20
+        ),
+        name="reduce_gradients",
+    )(*split, vectors)
+    return result[:6], result[6]
 
 
 def shards(
@@ -189,45 +442,18 @@
     ).reshape(rows, stretch, width)
     grad_input = jnp.where(widened[..., None], 0.0, d_input).astype(jnp.bfloat16)
     g_mask = jnp.sum(jnp.where(widened[..., None], d_input, 0.0), (0, 1))
-    matrices = (
-        g_query_weight,
-        g_key_weight,
-        g_value_weight,
-        g_output_weight,
-        g_inner_weight,
-        g_outer_weight,
-    )
-    partial_sums = (
-        lax.psum_scatter(matrices[0], "batch", scatter_dimension=0, tiled=True),
-        lax.psum_scatter(matrices[1], "batch", scatter_dimension=0, tiled=True),
-        lax.psum_scatter(matrices[2], "batch", scatter_dimension=0, tiled=True),
-        lax.psum_scatter(matrices[3], "batch", scatter_dimension=0, tiled=True),
-        lax.psum_scatter(matrices[4], "batch", scatter_dimension=0, tiled=True),
-        lax.psum_scatter(matrices[5], "batch", scatter_dimension=0, tiled=True),
-    )
-    summed = (
-        lax.psum_scatter(partial_sums[0], "seq", scatter_dimension=1, tiled=True),
-        lax.psum_scatter(partial_sums[1], "seq", scatter_dimension=1, tiled=True),
-        lax.psum_scatter(partial_sums[2], "seq", scatter_dimension=1, tiled=True),
-        lax.psum_scatter(partial_sums[3], "seq", scatter_dimension=1, tiled=True),
-        lax.psum_scatter(partial_sums[4], "seq", scatter_dimension=1, tiled=True),
-        lax.psum_scatter(partial_sums[5], "seq", scatter_dimension=1, tiled=True),
-    )
-    vectors = lax.psum(
-        (
-            g_mask,
-            g_query_bias,
-            g_value_bias,
-            g_output_bias,
-            d_mixing_gain,
-            d_mixing_shift,
-            g_inner_bias,
-            g_outer_bias,
-            d_final_gain,
-            d_final_shift,
-        ),
-        ("batch", "seq"),
-    )
+    small_vectors = jnp.stack(
+        [g_mask, g_query_bias, g_value_bias, g_output_bias, d_mixing_gain, d_mixing_shift]
+        + [g_inner_bias[i * width : (i + 1) * width] for i in range(4)]
+        + [g_outer_bias, d_final_gain, d_final_shift]
+    )
+    small_vectors = jnp.pad(small_vectors, ((0, 3), (0, 0)))
+    summed, vectors = reduce_gradients(
+        [g.astype(jnp.bfloat16) for g in (g_outer_weight, g_inner_weight, g_query_weight, g_key_weight, g_value_weight, g_output_weight)],
+        small_vectors,
+    )
+    summed = (summed[2], summed[3], summed[4], summed[5], summed[1], summed[0])
+    vectors = [vectors[i] for i in range(6)] + [vectors[6:10].reshape(-1)] + [vectors[i] for i in range(10, 13)]
     return (
         layer_out,
         grad_input,

time: 1020 us -> 408 us (0.40)
  waiting for transfers between devices: 705 us -> 46.2 us
  Pallas kernels: 0 us -> 106 us
  blocking collectives: 41.1 us -> 0 us
  matrix products: 171 us -> 153 us
    reduce_scatter x7 -> x0, waiting for transfers between devices: 607 us -> none  [the longest x1 166 us: shards(): lax.psum_scatter(matrices[5], 'batch', scatter_dimension=0, tiled=True)]
    pallas_call x0 -> x1, Pallas kernels: none -> 106 us  [reduce_gradients(): pl.pallas_call(reduce_body, out_shape=outs, in_specs=[pl.BlockSpec(memory...]
    unnamed x21 -> x4, waiting for transfers between devices: 66.6 us -> 0.07 us
    psum x1 -> x0, blocking collectives: 41.1 us -> none  [shards(): lax.psum((g_mask, g_query_bias, g_value_bias, g_output_bias, d_mixing_gai...]
    reduce_scatter x1, waiting for transfers between devices: 0.02 us -> 18.3 us  [shards(): lax.psum_scatter(d_value_part.reshape(rows, whole, width), 'seq', scatter...]
    unnamed x102 -> x135, local copies, waits for them, and re-layouts: 23.9 us -> 14.5 us
  transfers between devices with their start and end apart: 18 -> 6, of which waited for: 13 -> 4; matrix products, arithmetic and copies ran while one was open for 17% -> 26% of each run, Pallas kernels for 0% -> 0%
where the time goes in v1:
time: 408 us; the launch traced here: 404 us
  matrix products  153 us (38%)
  Pallas kernels  106 us (26%)
  local copies, waits for them, and re-layouts  60.5 us (15%)
  waiting for transfers between devices  46.2 us (11%)
  other arithmetic  19.5 us (5%)
  between operations  14.9 us (4%)
  starting transfers between devices  4.47 us (1%)
    pallas_call x1, Pallas kernels, reduce_gradients(): pl.pallas_call(reduce_body, out_shape=outs, in_specs=[pl.BlockSpec(memory...  106 us
    dot_general x1, matrix products, shards(): jnp.einsum('rhqk,rqhd->rkhd', d_raw, query_heads, preferred_element_type=...  35.8 us
    dot_general x1, matrix products, shards(): jnp.einsum('rhqk,rkhd->rqhd', d_raw, key_heads, preferred_element_type=jn...  34.8 us
    dot_general x6, matrix products, linear(): return jnp.dot(inputs, weight, preferred_element_type=jnp.float32)  23.9 us
    dot_general x6, matrix products, contract_rows(): lax.dot_general(left, right, (((0,), (0,)), ((), ())), preferred_element_...  20.4 us
    reduce_scatter x1, waiting for transfers between devices, shards(): lax.psum_scatter(d_value_part.reshape(rows, whole, width), 'seq', scatter...  18.3 us
    unnamed x135, local copies, waits for them, and re-layouts  14.5 us
    all_gather x1, waiting for transfers between devices, shards(): lax.all_gather(value_rows, 'seq', axis=1, tiled=True)  14.1 us
  transfers between devices with their start and end apart: 6, of which 4 were waited for; matrix products, arithmetic and copies ran while one was open for 26% of the time, Pallas kernels for 0%

profile of v1, /device:TPU:0, one launch (start us, length us, event | category | flops | bytes accessed | tf_op | source)
XLA Modules:
  0.0 403.8 jit_solution(1134974934595375867)
XLA Ops:
  9.5 3.0 collective-permute-start
  16.0 3.0 convolution_convert_fusion.5
  28.9 3.0 reshape.290
  34.0 13.6 %all-gather.5.cloned.1.call-done = bf16[3,512,768]{2,1,0:T(8,128)(2,1)} async-done(((bf16[3,128,768]{2,1,0:T(8,128)(2,1)}), bf16[3,512,768]{2,1,0:T(8,128)(2,1)}) %all-gather.5.cloned.1.call-update) | async-done | bytes 2359312 | tf_op jit(solution)/shard_map/all_gather | solution.py:347
  47.6 4.3 %copy.52 = bf16[3,512,768]{1,2,0:T(8,128)(2,1)} copy(bf16[3,512,768]{2,1,0:T(8,128)(2,1)} %all-gather.5.cloned.1.call-done) | data formatting | bytes 4718592 | tf_op jit(solution)/shard_map/all_gather | solution.py:347
  51.9 3.4 fusion.3
  59.7 14.1 %all-gather.3.cloned.1.call-done = bf16[3,512,768]{2,1,0:T(8,128)(2,1)} async-done(((bf16[3,128,768]{2,1,0:T(8,128)(2,1)}), bf16[3,512,768]{2,1,0:T(8,128)(2,1)}) %all-gather.3.cloned.1.call-update) | async-done | bytes 2359312 | tf_op jit(solution)/shard_map/all_gather | solution.py:348
  73.8 4.3 %copy.50 = bf16[3,512,768]{1,2,0:T(8,128)(2,1)} copy(bf16[3,512,768]{2,1,0:T(8,128)(2,1)} %all-gather.3.cloned.1.call-done) | data formatting | bytes 4718592 | tf_op jit(solution)/shard_map/all_gather | solution.py:348
  78.2 6.1 %fusion.34 = bf16[3,128,12,64]{1,3,2,0:T(8,128)(2,1)S(1)} fusion(bf16[3,512,12,64]{1,3,2,0:T(8,128)(2,1)} %bitcast.101, f32[3,12,128,512]{3,2,1,0:T(8,128)} %copy-done.1, f32[3,12,128]{2,1,0:T(8,128)} %copy-done.17, f32[3,12,128]{2,1,0:T(8,128)} %copy-done.15, pred[3,512]{1,0:T(4,128)(4,1)S(1)} %iota_compare_fusion), kind=kOutput, calls=%fused_computation.61 | convolution fusion | flops 314081280 | bytes 12424704 | tf_op jit(solution)/shard_map/rhqk,rkhd->rqhd/dot_general | solution.py:366
  86.1 14.1 %multiply_convert_fusion.1 = (bf16[384,3072]{1,0:T(8,128)(2,1)S(1)}, f32[384,3072]{1,0:T(8,128)S(1)}, f32[384,3072]{1,0:T(8,128)}) fusion(f32[3072]{0:T(1024)S(1)} %copy-done.33, bf16[768,3072]{1,0:T(8,128)(2,1)S(1)} %bitcast.129, f32[384,768]{1,0:T(8,128)S(1)} %get-tuple-element.108, f32[768]{0:T(1024)S(1)} %copy-done.42, ...), kind=kOutput, calls=%fused_computation.20 | convolution fusion | flops 1891270656 | bytes 17716224 | tf_op jit(solution)/shard_map/dot_general | solution.py:35
  105.8 5.4 %convert_reduce_fusion = (f32[3072]{0:T(1024)S(1)}, bf16[384,3072]{1,0:T(8,128)(2,1)S(1)}) fusion(f32[384,3072]{1,0:T(8,128)S(1)} %get-tuple-element.95, f32[384,3072]{1,0:T(8,128)} %get-tuple-element.109, bf16[384,768]{1,0:T(8,128)(2,1)S(1)} %get-tuple-element.83, bf16[3072,768]{1,0:T(8,128)(2,1)S(1)} %bitcast.127), kind=kOutput, calls=%fused_computation.16 | convolution fusion | flops 1830810624 | bytes 17117184 | tf_op jit(solution)/shard_map/dot_general | solution.py:39
  111.2 2.9 multiply_reduce_fusion.1
  122.4 6.7 %fusion.88 = f32[3,12,128,512]{3,2,1,0:T(8,128)} fusion(bf16[3,128,12,64]{1,3,2,0:T(8,128)(2,1)S(1)} %copy.56, bf16[3,512,12,64]{1,3,2,0:T(8,128)(2,1)} %bitcast.102), kind=kOutput, calls=%fused_computation.157 | convolution fusion | flops 301989888 | bytes 12386304 | tf_op jit(solution)/shard_map/rqhd,rkhd->rhqk/dot_general | solution.py:409
  129.1 35.8 %fusion.7 = f32[3,12,64,512]{3,2,1,0:T(8,128)} fusion(bf16[3,128,12,64]{1,3,2,0:T(8,128)(2,1)S(1)} %copy.53, f32[3,12,128,512]{3,2,1,0:T(8,128)} %fusion.88, f32[3,12,128,512]{3,2,1,0:T(8,128)} %copy-done.1, f32[3,12,128]{2,1,0:T(8,128)} %log_add_fusion, pred[3,512]{1,0:T(4,128)(4,1)S(1)} %iota_compare_fusion), kind=kOutput, calls=%fused_computation.11 | convolution fusion | flops 327947264 | bytes 24202752 | tf_op jit(solution)/shard_map/rhqk,rqhd->rkhd/dot_general | solution.py:416
  164.9 6.1 %copy.59 = f32[3,512,768]{2,1,0:T(8,128)} copy(f32[3,512,768]{1,2,0:T(8,128)} %bitcast.103) | data formatting | bytes 9437184 | tf_op jit(solution)/shard_map/reshape | solution.py:424
  171.8 8.6 %fusion.13 = f32[3,12,64,512]{3,2,1,0:T(8,128)} fusion(bf16[3,128,12,64]{1,3,2,0:T(8,128)(2,1)S(1)} %copy.56, f32[3,12,128,512]{3,2,1,0:T(8,128)} %copy-done.1, f32[3,12,128]{2,1,0:T(8,128)S(1)} %copy-done.16, pred[3,512]{1,0:T(4,128)(4,1)S(1)} %iota_compare_fusion), kind=kOutput, calls=%fused_computation.17 | convolution fusion | flops 311427072 | bytes 14765568 | tf_op jit(solution)/shard_map/rhqk,rqhd->rkhd/dot_general | solution.py:419
  180.3 6.3 %copy.61 = f32[3,512,768]{2,1,0:T(8,128)} copy(f32[3,512,768]{1,2,0:T(8,128)} %bitcast.98) | data formatting | bytes 9437184 | tf_op jit(solution)/shard_map/reshape | solution.py:427
  188.0 34.8 %convert_reduce_fusion.4 = (f32[12,64]{1,0:T(8,128)S(1)}, bf16[3,128,12,64]{1,3,2,0:T(8,128)(2,1)}) fusion(bf16[3,512,12,64]{1,3,2,0:T(8,128)(2,1)} %bitcast.100, f32[3,12,128,512]{3,2,1,0:T(8,128)} %fusion.88, f32[3,12,128]{2,1,0:T(8,128)S(1)} %copy-done.16, f32[3,12,128,512]{3,2,1,0:T(8,128)} %copy-done.1, pred[3,512]{1,0:T(4,128)(4,1)S(1)} %iota_compare_fusion), kind=kOutput, calls=%fused_computation.69 | convolution fusion | flops 328831232 | bytes 21846528 | tf_op jit(solution)/shard_map/rhqk,rkhd->rqhd/dot_general | solution.py:414
  230.4 3.4 convolution_convert_fusion.2
  238.6 4.3 %convolution_convert_fusion.1 = bf16[3072,768]{1,0:T(8,128)(2,1)} fusion(bf16[384,3072]{1,0:T(8,128)(2,1)S(1)} %copy-done.59, bf16[384,768]{1,0:T(8,128)(2,1)S(1)} %copy-done.13), kind=kOutput, calls=%fused_computation.14 | convolution fusion | flops 1814298624 | bytes 7667712 | tf_op jit(solution)/shard_map/dot_general | solution.py:45
  243.0 5.0 %convolution_convert_fusion = bf16[768,3072]{1,0:T(8,128)(2,1)} fusion(bf16[384,3072]{1,0:T(8,128)(2,1)S(1)} %copy-done.57, f32[384,768]{1,0:T(8,128)S(1)} %copy-done.3, f32[768]{0:T(1024)S(1)} %copy-done.43, f32[768]{0:T(1024)S(1)} %copy-done.28, f32[384]{0:T(512)S(1)} %copy-done.35, f32[384]{0:T(512)S(1)} %copy-done.21), kind=kOutput, calls=%fused_computation.13 | convolution fusion | flops 1815773184 | bytes 8266752 | tf_op jit(solution)/shard_map/dot_general | solution.py:45
  251.2 18.3 %reduce-scatter.5.cloned.1.call-done = f32[3,128,768]{2,1,0:T(8,128)} async-done(((f32[3,512,768]{2,1,0:T(8,128)}), f32[3,128,768]{2,1,0:T(8,128)}) %reduce-scatter.5.cloned.1.call-update) | async-done | bytes 1179664 | tf_op jit(solution)/shard_map/reduce_scatter | solution.py:426
  271.0 2.9 bitcast_convert_fusion
  277.6 105.6 %reduce_gradients.1 = (f32[384,192]{1,0:T(8,128)}, f32[96,768]{1,0:T(8,128)}, f32[96,192]{1,0:T(8,128)}, f32[96,192]{1,0:T(8,128)}, f32[96,192]{1,0:T(8,128)}, /*index=5*/f32[96,192]{1,0:T(8,128)}, f32[16,768]{1,0:T(8,128)}) custom-call(bf16[2,2,2,2,192,768]{5,4,3,2,1,0:T(8,128)(2,1)} %bitcast.104, bf16[2,2,2,96,3072]{4,3,2,1,0:T(8,128)(2,1)} %bitcast.105, ...), custom_call_target="tpu_custom_call" | custom-call | tf_op jit(solution)/shard_map/reduce_gradients/pallas_call | solution.py:289
  (221 shorter events, 73.9 us)
Async XLA Ops:
  7.2 15.8 %copy-start.48 = (bf16[768]{0:T(1024)(128)(2,1)S(1)}, bf16[768]{0:T(1024)(128)(2,1)}, u32[]{:S(2)}) copy-start(bf16[768]{0:T(1024)(128)(2,1)} %param.28) | copy-start | bytes 4612
  7.3 16.4 %copy-start.49 = (bf16[768]{0:T(1024)(128)(2,1)S(1)}, bf16[768]{0:T(1024)(128)(2,1)}, u32[]{:S(2)}) copy-start(bf16[768]{0:T(1024)(128)(2,1)} %param.35) | copy-start | bytes 4612
  7.3 17.0 %copy-start.50 = (bf16[768]{0:T(1024)(128)(2,1)S(1)}, bf16[768]{0:T(1024)(128)(2,1)}, u32[]{:S(2)}) copy-start(bf16[768]{0:T(1024)(128)(2,1)} %param.34) | copy-start | bytes 4612
  7.3 17.0 %copy-start.51 = (bf16[768]{0:T(1024)(128)(2,1)S(1)}, bf16[768]{0:T(1024)(128)(2,1)}, u32[]{:S(2)}) copy-start(bf16[768]{0:T(1024)(128)(2,1)} %param.40) | copy-start | bytes 4612
  7.3 17.0 %copy-start.52 = (bf16[768]{0:T(1024)(128)(2,1)S(1)}, bf16[768]{0:T(1024)(128)(2,1)}, u32[]{:S(2)}) copy-start(bf16[768]{0:T(1024)(128)(2,1)} %param.41) | copy-start | bytes 4612
  7.3 17.0 %copy-start.53 = (s32[3]{0:T(128)S(1)}, s32[3]{0:T(128)}, u32[]{:S(2)}) copy-start(s32[3]{0:T(128)} %param.24) | copy-start | bytes 40
  7.3 40.3 %all-gather.5.cloned.1.call-start = ((), (), s32[]{:S(2)}) async-start(), calls=%async_computation.3 | async-start | bytes 2949120 | tf_op jit(solution)/shard_map/all_gather | solution.py:347
  8.2 5.0 %collective-permute-start.1 = (s32[3,5]{1,0:T(4,128)S(1)}, s32[3,5]{1,0:T(4,128)S(1)}, u32[]{:S(2)}, u32[]{:S(2)}) collective-permute-start(s32[3,5]{1,0:T(4,128)S(1)} %get-tuple-element.104), channel_id=1, source_target_pairs={{1,0},{2,1},{3,2},{5,4},{6,5},{7,6},{9,8},{10,9},{11,10},{13,12},{... | collective-permute-start | bytes 188 | tf_op jit(solution)/shard_map/ppermute | solution.py:23
  9.5 3.8 collective-permute-start
  19.0 54.9 %all-gather.3.cloned.1.call-start = ((), (), s32[]{:S(2)}) async-start(), calls=%async_computation.2 | async-start | bytes 2949120 | tf_op jit(solution)/shard_map/all_gather | solution.py:348
  21.2 226.8 %reduce-scatter.3.cloned.1.call-start = ((), (), s32[]{:S(2)}) async-start(), calls=%async_computation.4 | async-start | bytes 5898240 | tf_op jit(solution)/shard_map/reduce_scatter | solution.py:423
  24.3 75.9 %copy-start.26 = (f32[768]{0:T(1024)}, f32[768]{0:T(1024)S(1)}, u32[]{:S(2)}) copy-start(f32[768]{0:T(1024)S(1)} %convert_element_type.154) | copy-start | bytes 9220
  59.1 19.0 %copy-start.17 = (f32[3,12,128]{2,1,0:T(8,128)}, f32[3,12,128]{2,1,0:T(8,128)S(1)}, u32[]{:S(2)}) copy-start(f32[3,12,128]{2,1,0:T(8,128)S(1)} %fusion.2) | copy-start | bytes 55300
  84.9 15.3 %copy-start.8 = (bf16[3,128,12,64]{1,0,3,2:T(4,128)(2,1)}, bf16[3,128,12,64]{1,0,3,2:T(4,128)(2,1)S(1)}, u32[]{:S(2)}) copy-start(bf16[3,128,12,64]{1,0,3,2:T(4,128)(2,1)S(1)} %copy.54) | copy-start | bytes 1769476
  85.7 28.4 %copy-start.2 = (f32[384,768]{1,0:T(8,128)}, f32[384,768]{1,0:T(8,128)S(1)}, u32[]{:S(2)}) copy-start(f32[384,768]{1,0:T(8,128)S(1)} %get-tuple-element.108) | copy-start | bytes 3538948
  85.7 28.4 %copy-start.20 = (f32[384]{0:T(512)}, f32[384]{0:T(512)S(1)}, u32[]{:S(2)}) copy-start(f32[384]{0:T(512)S(1)} %broadcast_multiply_fusion.1) | copy-start | bytes 4612
  86.0 28.1 %copy-start.34 = (f32[384]{0:T(512)}, f32[384]{0:T(512)S(1)}, u32[]{:S(2)}) copy-start(f32[384]{0:T(512)S(1)} %fusion.61) | copy-start | bytes 4612
  171.0 98.5 %reduce-scatter.5.cloned.1.call-start = ((), (), s32[]{:S(2)}) async-start(), calls=%async_computation.5 | async-start | bytes 5898240 | tf_op jit(solution)/shard_map/reduce_scatter | solution.py:426
  187.9 37.2 %copy-start.25 = (f32[768]{0:T(1024)S(1)}, f32[768]{0:T(1024)}, u32[]{:S(2)}) copy-start(f32[768]{0:T(1024)} %get-tuple-element.86) | copy-start | bytes 9220
  187.9 37.8 %copy-start.41 = (f32[768]{0:T(1024)S(1)}, f32[768]{0:T(1024)}, u32[]{:S(2)}) copy-start(f32[768]{0:T(1024)} %get-tuple-element.70) | copy-start | bytes 9220
  188.0 38.4 %copy-start.40 = (f32[768]{0:T(1024)S(1)}, f32[768]{0:T(1024)}, u32[]{:S(2)}) copy-start(f32[768]{0:T(1024)} %get-tuple-element.72) | copy-start | bytes 9220
  188.0 41.3 %copy-start.24 = (f32[768]{0:T(1024)S(1)}, f32[768]{0:T(1024)}, u32[]{:S(2)}) copy-start(f32[768]{0:T(1024)} %get-tuple-element.82) | copy-start | bytes 9220
  188.0 41.9 %copy-start.23 = (f32[768]{0:T(1024)S(1)}, f32[768]{0:T(1024)}, u32[]{:S(2)}) copy-start(f32[768]{0:T(1024)} %get-tuple-element.68) | copy-start | bytes 9220
  277.6 108.1 %copy-start.39 = (pred[3,128]{1,0:T(4,128)(4,1)S(1)}, pred[3,128]{1,0:T(4,128)(4,1)}, u32[]{:S(2)}) copy-start(pred[3,128]{1,0:T(4,128)(4,1)} %copy-done.37) | copy-start | bytes 1156
  (46 other events, 320.8 us)
Sparse Core Ops, SparseCore 0:
  19.1 28.4 all-gather.4
  49.7 24.0 all-gather.2
  171.2 47.8 reduce-scatter.2
  221.6 47.8 reduce-scatter.4

commit v2 on v0

--- a/solution.py
+++ b/solution.py
@@ -1,11 +1,895 @@
 import jax
 import jax.numpy as jnp
 from jax import lax
+from jax.experimental import pallas as pl
+from jax.experimental.pallas import tpu as pltpu
 from jax.sharding import PartitionSpec as P
 
 HEADS = 12
 HEAD_DIM = 64
 WIDEN = 5
+
+MESH = pl.DeviceIdType.MESH
+F32 = jnp.float32
+BF16 = jnp.bfloat16
+ROOT_HALF = 0.7071067811865476
+DENSITY = 0.3989422804014327
+
+
+def mm(a, b):
+    return jnp.dot(a, b, preferred_element_type=F32)
+
+
+def mm_t(a, b):
+    return lax.dot_general(a, b, (((1,), (1,)), ((), ())), preferred_element_type=F32)
+
+
+def mm_tl(a, b):
+    return lax.dot_general(a, b, (((0,), (0,)), ((), ())), preferred_element_type=F32)
+
+
+def fold(v):
+    return jnp.sum(v.reshape(v.shape[0] // 8, 8, v.shape[1]), 0)
+
+
+def loop(count, body):
+    def step(i, carry):
+        body(i)
+        return carry
+
+    lax.fori_loop(0, count, step, 0)
+
+
+def aligned(i, size):
+    return pl.ds(pl.multiple_of(i * size, size), size)
+
+
+def places():
+    b, s = lax.axis_index("batch"), lax.axis_index("seq")
+    x, zlo, zhi = lax.rem(b, 2), lax.rem(b // 2, 2), b // 4
+    core, y = lax.rem(s, 2), s // 2
+    spot = {"core": core, "x": x, "y": y, "zlo": zlo, "zhi": zhi}
+    peer = {
+        "core": (b, s + 1 - 2 * core),
+        "y": (b, s + 2 - 4 * y),
+        "x": (b + 1 - 2 * x, s),
+        "zlo": (b + 2 - 4 * zlo, s),
+        "zhi": (b + 4 - 8 * zhi, s),
+        "far": (b, 3 - s),
+    }
+    return spot, peer
+
+
+class Unit:
+    def __init__(self, number, order, both, inbox, sends, recvs, spot, peer):
+        self.number, self.order, self.both, self.inbox = number, order, both, inbox
+        self.sends, self.recvs, self.spot, self.peer = sends, recvs, spot, peer
+        self.own = both.at[spot["core"]]
+
+    def axis(self, phase):
+        return ("core", *self.order, "zlo", "zhi")[phase]
+
+    def where(self, phase, stays):
+        spot = self.spot
+        first = self.order[0]
+        here = lambda name: spot[name] if stays else 1 - spot[name]
+        if phase == 1 and first == "x":
+            return (slice(None), slice(None), slice(None), here("x"))
+        if phase == 1:
+            return (here("y"),)
+        if phase == 2 and first == "x":
+            return (here("y"), slice(None), slice(None), spot["x"])
+        if phase == 2:
+            return (spot["y"], slice(None), slice(None), here("x"))
+        if phase == 3:
+            return (spot["y"], slice(None), here("zlo"), spot["x"])
+        return (spot["y"], here("zhi"), spot["zlo"], spot["x"])
+
+    def copy(self, phase):
+        if phase == 0:
+            source = self.both.at[1 - self.spot["core"]]
+        else:
+            source = self.own.at[self.where(phase, False)]
+        return pltpu.make_async_remote_copy(
+            src_ref=source,
+            dst_ref=self.inbox[phase],
+            send_sem=self.sends.at[self.number, phase],
+            recv_sem=self.recvs.at[self.number, phase],
+            device_id=self.peer[self.axis(phase)],
+            device_id_type=MESH,
+        )
+
+    def start(self, phase):
+        self.copy(phase).start()
+
+    def finish(self, phase):
+        self.copy(phase).wait()
+        came = self.inbox[phase]
+        target = self.own if phase == 0 else self.own.at[self.where(phase, True)]
+        lead = came.shape[:-2]
+        count = 1
+        for size in lead:
+            count *= size
+
+        def body(n):
+            place = []
+            for size in reversed(lead):
+                place.append(lax.rem(n, size))
+                n = n // size
+            place = tuple(reversed(place))
+            target[place] = target[place] + came[place]
+
+        loop(count, body)
+
+    def step(self, phase):
+        self.finish(phase)
+        self.start(phase + 1)
+
+
+ORDERS = (("x", "y"), ("y", "x"), ("x", "y"), ("y", "x"), ("x", "y"), ("y", "x"))
+SLOTS = 3
+
+
+def layer_body(
+    hidden,
+    cotangent,
+    query_weight,
+    key_weight,
+    value_weight,
+    output_weight,
+    inner_weight,
+    outer_weight,
+    span,
+    params,
+    lengths,
+    repeats,
+    layer_out,
+    grad_input,
+    probs_out,
+    out_query,
+    out_key,
+    out_value,
+    out_output,
+    out_inner,
+    out_outer,
+    out_vectors,
+    wi,
+    wf,
+    wq,
+    wk,
+    wv,
+    wo,
+    x_all,
+    k_all,
+    v_all,
+    q_own,
+    mixed,
+    region,
+    first_low,
+    norm_one,
+    spread_one,
+    total,
+    d_res,
+    d_outer,
+    d_att,
+    masks,
+    wide,
+    inner_sums,
+    grads,
+    in0,
+    in1,
+    in2,
+    in3,
+    in4,
+    in5,
+    d_in0,
+    d_in1,
+    vec,
+    vec_came,
+    sends,
+    recvs,
+    x_send,
+    x_recv,
+    m_send,
+    m_recv,
+    v_send,
+    v_recv,
+    local,
+    credit,
+):
+    spot, peer = places()
+    core, y = spot["core"], spot["y"]
+    me = 2 * y + core
+    sibling = 2 * y + 1 - core
+    across = 2 * (1 - y) + core
+
+    weight_loads = {}
+
+    def load(name, number, source, target):
+        copy = pltpu.make_async_copy(source, target, local.at[number])
+        copy.start()
+        weight_loads[name] = copy
+
+    load("hidden", 0, hidden, x_all.at[:, aligned(me, 128)])
+    load("key", 1, key_weight, wk)
+    load("value", 2, value_weight, wv)
+    load("query", 3, query_weight, wq)
+    load("output", 4, output_weight, wo)
+    for j in range(4):
+        load(f"inner{j}", 5 + j, inner_weight.at[:, pl.ds(768 * j, 768)], wi.at[pl.ds(768 * j, 768)])
+    load("outer", 9, outer_weight, wf)
+    load("cotangent", 10, cotangent, d_outer)
+
+    names = ("core", "x", "y", "zlo", "zhi", "far")
+    barrier = pltpu.get_barrier_semaphore()
+    for name in names:
+        pl.semaphore_signal(barrier, inc=1, device_id=peer[name], device_id_type=MESH)
+    pl.semaphore_wait(barrier, len(names))
+
+    masks[me] = jnp.zeros((8, 128), jnp.int32)
+    masks[me, 0:3] = span[...]
+    mask_copies = []
+    for i, name in enumerate(("core", "y", "far")):
+        copy = pltpu.make_async_remote_copy(
+            src_ref=masks.at[me],
+            dst_ref=masks.at[me],
+            send_sem=m_send.at[i],
+            recv_sem=m_recv.at[i],
+            device_id=peer[name],
+            device_id_type=MESH,
+        )
+        copy.start()
+        mask_copies.append(copy)
+
+    def x_copy(kind, r):
+        source = hidden.at[r] if kind < 2 else x_all.at[r, aligned(across, 128)]
+        slot = me if kind < 2 else across
+        return pltpu.make_async_remote_copy(
+            src_ref=source,
+            dst_ref=x_all.at[r, aligned(slot, 128)],
+            send_sem=x_send.at[kind, r],
+            recv_sem=x_recv.at[kind, r],
+            device_id=peer["y" if kind == 0 else "core"],
+            device_id_type=MESH,
+        )
+
+    for r in range(3):
+        x_copy(0, r).start()
+        x_copy(1, r).start()
+
+    for copy in mask_copies:
+        copy.wait()
+    span_all = jnp.concatenate([masks[s].astype(F32) for s in range(4)], axis=1)
+    lane = lax.broadcasted_iota(jnp.int32, span_all.shape, 1)
+    window = span_all
+    for d in range(1, WIDEN + 1):
+        window = jnp.maximum(window, jnp.where(lane >= d, pltpu.roll(span_all, d, 1), 0.0))
+        window = jnp.maximum(
+            window, jnp.where(lane < 512 - d, pltpu.roll(span_all, 512 - d, 1), 0.0)
+        )
+    wide[...] = window.T
+
+    weight_loads["hidden"].wait()
+    weight_loads["key"].wait()
+    weight_loads["value"].wait()
+    weight_loads["query"].wait()
+    half = lax.broadcasted_iota(jnp.int32, (128, 128), 1) < HEAD_DIM
+    zero = jnp.zeros((128, 128), BF16)
+
+    def stacked(pair):
+        return jnp.concatenate([jnp.where(half, pair, zero), jnp.where(half, zero, pair)], 0)
+
+    def unstacked(both):
+        return jnp.where(half, both[:128], both[128:])
+
+    mask_row = params[0:1]
+    spills = []
+    for r in range(3):
+        x_copy(0, r).wait_recv()
+        x_copy(2, r).start()
+        x_copy(1, r).wait_recv()
+        x_copy(2, r).wait()
+        x_copy(0, r).wait_send()
+        x_copy(1, r).wait_send()
+
+        def put_mask(i):
+            rows = aligned(i, 128)
+            chosen = wide[rows, r : r + 1] > 0.5
+            kept = x_all[r, rows].astype(F32)
+            x_all[r, rows] = jnp.where(chosen, mask_row, kept).astype(BF16)
+
+        loop(4, put_mask)
+
+        def project(n):
+            cols = aligned(n, 256)
+            x_row = x_all[r]
+            k_all[r, :, cols] = mm(x_row, wk[:, cols]).astype(BF16)
+            v_all[r, :, cols] = (mm(x_row, wv[:, cols]) + params[2:3, cols]).astype(BF16)
+            x_own = x_all[r, aligned(me, 128)]
+            q_own[pl.ds(128 * r, 128), cols] = (
+                mm(x_own, wq[:, cols]) + params[1:2, cols]
+            ).astype(BF16)
+
+        loop(3, project)
+        key_live = lax.broadcasted_iota(jnp.int32, (1, 512), 1) < lengths[r]
+
+        def attend(p):
+            cols = aligned(p, 128)
+            queries = stacked(q_own[pl.ds(128 * r, 128), cols] * BF16(HEAD_DIM**-0.5))
+            logits = mm_t(queries, k_all[r, :, cols])
+            logits = jnp.where(key_live, logits, -1e30)
+            expd = jnp.exp(logits - jnp.max(logits, -1, keepdims=True))
+            probs = (expd / jnp.sum(expd, -1, keepdims=True)).astype(BF16)
+            base = r * 6 + p
+            region[aligned(2 * base, 256)] = probs[:, :256]
+            region[aligned(2 * base + 1, 256)] = probs[:, 256:]
+            out = mm(probs, v_all[r, :, cols])
+            mixed[pl.ds(128 * r, 128), cols] = unstacked(out).astype(BF16)
+
+        loop(6, attend)
+        rows = pl.ds(3072 * r, 3072)
+        spill = pltpu.make_async_copy(region.at[rows], probs_out.at[rows], local.at[11 + r])
+        spill.start()
+        spills.append(spill)
+
+    weight_loads["output"].wait()
+
+    def first_norm(i):
+        rows = aligned(i, 128)
+        attended = mm(mixed[rows], wo[...]) + params[3:4]
+        value = x_all[i, aligned(me, 128)].astype(F32) + attended
+        center = value - jnp.mean(value, -1, keepdims=True)
+        scale = lax.rsqrt(jnp.mean(center * center, -1, keepdims=True) + 1e-5)
+        norm = center * scale
+        norm_one[rows] = norm
+        spread_one[rows] = scale
+        first_low[rows] = (norm * params[4:5] + params[5:6]).astype(BF16)
+
+    loop(3, first_norm)
+    for spill in spills:
+        spill.wait()
+    for j in range(4):
+        weight_loads[f"inner{j}"].wait()
+
+    def hidden_units(j):
+        inner = mm(
+            first_low[...], wi[pl.ds((j // 3) * 768, 768), aligned(lax.rem(j, 3), 256)]
+        ) + params[pl.ds(6 + j // 3, 1), aligned(lax.rem(j, 3), 256)]
+        below = 0.5 * (1.0 + lax.erf(inner * ROOT_HALF))
+        slope = below + inner * (DENSITY * jnp.exp(-0.5 * inner * inner))
+        region[aligned(j, 384)] = (inner * below).astype(BF16)
+        region[aligned(12 + j, 384)] = slope.astype(BF16)
+
+    loop(12, hidden_units)
+    weight_loads["outer"].wait()
+    weight_loads["cotangent"].wait()
+
+    def panels(first, count):
+        return jnp.concatenate(
+            [region[pl.ds(384 * j, 384)] for j in range(first, first + count)], axis=1
+        )
+
+    def project_out(n):
+        cols = aligned(n, 256)
+        total[:, cols] = mm(panels(0, 12), wf[:, cols])
+
+    loop(3, project_out)
+
+    def last_norm(i, sums):
+        rows = aligned(i, 64)
+        first = norm_one[rows] * params[4:5] + params[5:6]
+        value = first + (total[rows] + params[10:11])
+        center = value - jnp.mean(value, -1, keepdims=True)
+        scale = lax.rsqrt(jnp.mean(center * center, -1, keepdims=True) + 1e-5)
+        norm = center * scale
+        d_att[rows] = (norm * params[11:12] + params[12:13]).astype(BF16)
+        r = i // 2
+        position = lax.broadcasted_iota(jnp.int32, (64, 1), 0) + lax.rem(i, 2) * 64 + me * 128
+        weight = jnp.where(position < lengths[r], repeats[r].astype(F32), 0.0)
+        d_final = d_outer[rows].astype(F32) * weight
+        d_norm = d_final * params[11:12]
+        d_two = scale * (
+            d_norm
+            - jnp.mean(d_norm, -1, keepdims=True)
+            - norm * jnp.mean(d_norm * norm, -1, keepdims=True)
+        )
+        d_res[rows] = d_two
+        low = d_two.astype(BF16)
+        d_outer[rows] = low
+        return (
+            sums[0] + fold(d_final * norm),
+            sums[1] + fold(d_final),
+            sums[2] + fold(low.astype(F32)),
+        )
+
+    nothing = jnp.zeros((8, 768), F32)
+
+    def put_sum(row, value):
+        vec[0, row : row + 1] = jnp.sum(value, 0, keepdims=True)
+
+    vec[0] = jnp.zeros((16, 768), F32)
+    sums = lax.fori_loop(0, 6, last_norm, (nothing, nothing, nothing))
+    put_sum(11, sums[0])
+    put_sum(12, sums[1])
+    put_sum(10, sums[2])
+    out_copy = pltpu.make_async_copy(
+        d_att, layer_out, local.at[14]
+    )
+    out_copy.start()
+
+    units = []
+    for u in range(6):
+        inbox = [in0.at[u % SLOTS], in1.at[u], in2.at[u], in3.at[u], in4.at[u]]
+        units.append(Unit(u, ORDERS[u], grads.at[u], inbox, sends, recvs, spot, peer))
+
+    def free_slot():
+        pl.semaphore_signal(credit, inc=1, device_id=peer["core"], device_id_type=MESH)
+
+    def claim_slot():
+        pl.semaphore_wait(credit, 1)
+
+    def outer_grads(z):
+        for x in range(2):
+            cols = [region[pl.ds(pl.multiple_of((3 * z + j) * 384, 384), 384)] for j in range(3)]
+            part = jnp.concatenate(cols, axis=1)[:, 384 * x : 384 * x + 384]
+            grad = mm_tl(part, d_outer[...]).astype(BF16)
+            for h in range(2):
+                for i in range(2):
+                    for side in range(2):
+                        rows = (h * 2 + i) * 96
+                        grads[i, h, side, z // 2, lax.rem(z, 2), x] = grad[
+                            rows : rows + 96, side * 384 : side * 384 + 384
+                        ]
+
+    loop(4, outer_grads)
+    units[0].start(0)
+    units[1].start(0)
+
+    def d_hidden_units(j):
+        d_act = mm_t(d_outer[...], wf[aligned(j, 256)])
+        place = aligned(12 + j, 384)
+        low = (d_act * region[place].astype(F32)).astype(BF16)
+        region[place] = low
+        inner_sums[j] = fold(low.astype(F32))
+
+    loop(12, d_hidden_units)
+
+    def inner_grads(s):
+        cols = [region[pl.ds(pl.multiple_of((12 + 3 * s + j) * 384, 384), 384)] for j in range(3)]
+        grad = mm_tl(first_low[...], jnp.concatenate(cols, axis=1)).astype(BF16)
+        for b in range(8):
+            for i in range(2):
+                grads[2 + i, lax.rem(s, 2), s // 2, b // 4, (b // 2) % 2, b % 2] = grad[
+                    96 * b : 96 * b + 96, 384 * i : 384 * i + 384
+                ]
+
+    loop(4, inner_grads)
+    units[2].start(0)
+    for u in range(2):
+        units[u].step(0)
+        if u == 0:
+            free_slot()
+            claim_slot()
+            units[3].start(0)
+        else:
+            free_slot()
+
+    def d_first_part(n):
+        cols = aligned(n, 256)
+        acc = None
+        for s in range(4):
+            d_inner = panels(12 + 3 * s, 3)
+            term = mm_t(d_inner, wi[pl.ds(pl.multiple_of(s * 768 + n * 256, 256), 256)])
+            acc = term if acc is None else acc + term
+        total[:, cols] = acc
+
+    loop(3, d_first_part)
+    for j in range(12):
+        vec[0, 6 + j // 3 : 7 + j // 3, (j % 3) * 256 : (j % 3) * 256 + 256] = jnp.sum(
+            inner_sums[j], 0, keepdims=True
+        )
+    refills = []
+    for r in range(3):
+        rows = pl.ds(3072 * r, 3072)
+        refill = pltpu.make_async_copy(probs_out.at[rows], region.at[rows], local.at[15 + r])
+        refill.start()
+        refills.append(refill)
+    out_copy.wait()
+
+    def first_norm_back(i, sums):
+        rows = aligned(i, 64)
+        d_first = total[rows] + d_res[rows]
+        norm = norm_one[rows]
+        d_norm = d_first * params[4:5]
+        d_one = spread_one[rows] * (
+            d_norm
+            - jnp.mean(d_norm, -1, keepdims=True)
+            - norm * jnp.mean(d_norm * norm, -1, keepdims=True)
+        )
+        d_res[rows] = d_one
+        low = d_one.astype(BF16)
+        d_att[rows] = low
+        return (
+            sums[0] + fold(d_first * norm),
+            sums[1] + fold(d_first),
+            sums[2] + fold(low.astype(F32)),
+        )
+
+    sums = lax.fori_loop(0, 6, first_norm_back, (nothing, nothing, nothing))
+    put_sum(4, sums[0])
+    put_sum(5, sums[1])
+    put_sum(3, sums[2])
+
+    def square_grads(u, lower, left, right):
+        for m in range(2):
+            grad = mm_tl(left(m), right).astype(BF16)
+            for b in range(4):
+                for h in range(2):
+                    for side in range(2):
+                        rows = b * 96 + h * 48
+                        grads[u, h, side, m, b // 2, b % 2, pl.ds(lower * 48, 48)] = grad[
+                            rows : rows + 48, side * 384 : side * 384 + 384
+                        ]
+
+    square_grads(4, 0, lambda m: mixed[:, 384 * m : 384 * m + 384], d_att[...])
+
+    def d_mixed_part(i):
+        rows = aligned(i, 128)
+        mixed[rows] = mm_t(d_att[rows], wo[...]).astype(BF16)
+
+    loop(3, d_mixed_part)
+    units[2].step(0)
+    free_slot()
+    units[3].step(0)
+
+    for r in range(3):
+        refills[r].wait()
+
+        def attend_back(p):
+            cols = aligned(p, 128)
+            own_rows = pl.ds(128 * r, 128)
+            base = r * 6 + p
+            queries = stacked(q_own[own_rows, cols] * BF16(HEAD_DIM**-0.5))
+            d_mix = stacked(mixed[own_rows, cols])
+            low_probs = jnp.concatenate(
+                [region[aligned(2 * base, 256)], region[aligned(2 * base + 1, 256)]], axis=1
+            )
+            d_probs = mm_t(d_mix, v_all[r, :, cols])
+            probs = low_probs.astype(F32)
+            weighted = probs * d_probs
+            d_raw = (weighted - probs * jnp.sum(weighted, -1, keepdims=True)).astype(BF16)
+            d_query = mm(d_raw, k_all[r, :, cols]) * HEAD_DIM**-0.5
+            q_own[own_rows, cols] = unstacked(d_query).astype(BF16)
+            wi[pl.ds(512 * r, 512), cols] = mm_tl(d_raw, queries).astype(BF16)
+            wi[pl.ds(1536 + 512 * r, 512), cols] = mm_tl(low_probs, d_mix).astype(BF16)
+
+        loop(6, attend_back)
+        if r == 0:
+            units[0].step(1)
+            units[1].step(1)
+        elif r == 1:
+            units[0].step(2)
+            units[1].step(2)
+        else:
+            units[2].step(1)
+            units[3].step(1)
+
+    def own_inputs(m):
+        return jnp.concatenate(
+            [x_all[r, aligned(me, 128), pl.ds(384 * m, 384)] for r in range(3)], 0
+        )
+
+    def all_inputs(m):
+        return jnp.concatenate([x_all[r, :, pl.ds(384 * m, 384)] for r in range(3)], 0)
+
+    square_grads(4, 1, own_inputs, q_own[...])
+    claim_slot()
+    units[4].start(0)
+    square_grads(5, 0, all_inputs, wi[pl.ds(0, 1536)])
+    square_grads(5, 1, all_inputs, wi[pl.ds(1536, 1536)])
+    claim_slot()
+    units[5].start(0)
+    put_sum(1, fold(q_own[...].astype(F32)))
+
+    def value_sum(i, acc):
+        return acc + fold(wi[pl.ds(pl.multiple_of(1536 + i * 128, 128), 128)].astype(F32))
+
+    put_sum(2, lax.fori_loop(0, 12, value_sum, nothing))
+    units[0].step(3)
+    units[1].step(3)
+
+    mask_sum = nothing
+    for r in range(3):
+
+        def d_in_part(s, acc):
+            part = mm_t(wi[pl.ds(pl.multiple_of(512 * r + s * 128, 128), 128)], wk[...]) + mm_t(
+                wi[pl.ds(pl.multiple_of(1536 + 512 * r + s * 128, 128), 128)], wv[...]
+            )
+            chosen = wide[aligned(s, 128), r : r + 1]
+            wf[pl.ds(pl.multiple_of(s * 384 + r * 128, 128), 128)] = part.astype(BF16)
+            return acc + fold(part * chosen)
+
+        mask_sum = lax.fori_loop(0, 4, d_in_part, mask_sum)
+
+    def d_in_copy(i):
+        if i < 2:
+            piece, target, name = 2 * i + 1 - core, d_in0.at[i], "core"
+        else:
+            piece, target, name = across, d_in1, "y"
+        return pltpu.make_async_remote_copy(
+            src_ref=wf.at[aligned(piece, 384)],
+            dst_ref=target,
+            send_sem=x_send.at[3, i],
+            recv_sem=x_recv.at[3, i],
+            device_id=peer[name],
+            device_id_type=MESH,
+        )
+
+    d_in_copy(0).start()
+    d_in_copy(1).start()
+
+    def own_part(i, acc):
+        rows = aligned(i, 128)
+        part = d_res[rows] + mm_t(q_own[rows], wq[...])
+        d_res[rows] = part
+        chosen = wide[aligned(me, 128)]
+        chosen = jnp.where(i == 0, chosen[:, 0:1], jnp.where(i == 1, chosen[:, 1:2], chosen[:, 2:3]))
+        return acc + fold(part * chosen)
+
+    put_sum(0, lax.fori_loop(0, 3, own_part, mask_sum))
+
+    def vector_copy(phase):
+        return pltpu.make_async_remote_copy(
+            src_ref=vec.at[phase],
+            dst_ref=vec_came.at[phase],
+            send_sem=v_send.at[phase],
+            recv_sem=v_recv.at[phase],
+            device_id=peer[names[phase]],
+            device_id_type=MESH,
+        )
+
+    def vector_step(phase):
+        vector_copy(phase).wait()
+        vec[phase + 1] = vec[phase] + vec_came[phase]
+        if phase < 4:
+            vector_copy(phase + 1).start()
+
+    vector_copy(0).start()
+    d_in_copy(0).wait()
+    d_in_copy(1).wait()
+
+    def add_across(i):
+        rows = pl.ds(pl.multiple_of(across * 384 + i * 128, 128), 128)
+        wf[rows] = wf[rows] + d_in0[1 - y, aligned(i, 128)]
+
+    loop(3, add_across)
+    d_in_copy(2).start()
+    units[4].step(0)
+    units[5].step(0)
+    vector_step(0)
+    units[2].step(2)
+    units[3].step(2)
+    vector_step(1)
+    units[4].step(1)
+    units[5].step(1)
+    vector_step(2)
+    units[2].step(3)
+    units[3].step(3)
+    units[4].step(2)
+    units[5].step(2)
+    vector_step(3)
+
+    mine = (y, spot["zhi"], spot["zlo"], spot["x"])
+
+    def swap_copy(u):
+        return pltpu.make_async_remote_copy(
+            src_ref=units[u].own.at[mine],
+            dst_ref=in5.at[u],
+            send_sem=sends.at[u, 5],
+            recv_sem=recvs.at[u, 5],
+            device_id=peer["core"],
+            device_id_type=MESH,
+        )
+
+    def close(u):
+        units[u].copy(4).wait()
+        result = units[u].own[mine].astype(F32) + in4[u].astype(F32)
+        if u == 2 or u == 3:
+            out_inner[:, pl.ds(384 * (u - 2), 384)] = result
+            return
+        units[u].own[mine] = result.astype(BF16)
+        swap_copy(u).start()
+        put_half(u, core, result)
+
+    def put_half(u, side, value):
+        value = jnp.where(core == 0, value[:, :192], pltpu.roll(value, 192, 1)[:, :192])
+        if u < 2:
+            out_outer[pl.ds(pl.multiple_of(side * 192 + u * 96, 96), 96)] = value
+            return
+        targets = (out_output, out_query) if u == 4 else (out_key, out_value)
+        for i, target in enumerate(targets):
+            target[pl.ds(pl.multiple_of(side * 48, 48), 48)] = value[48 * i : 48 * i + 48]
+
+    for u in range(4):
+        close(u)
+    units[4].step(3)
+    units[5].step(3)
+
+    d_in_copy(2).wait()
+
+    def finish_input(i):
+        rows = aligned(i, 128)
+        mine = pl.ds(pl.multiple_of(me * 384 + i * 128, 128), 128)
+        value = (
+            d_res[rows]
+            + wf[mine].astype(F32)
+            + d_in0[y, rows].astype(F32)
+            + d_in1[rows].astype(F32)
+        )
+        chosen = wide[aligned(me, 128)]
+        chosen = jnp.where(i == 0, chosen[:, 0:1], jnp.where(i == 1, chosen[:, 1:2], chosen[:, 2:3]))
+        d_att[rows] = jnp.where(chosen > 0.5, 0.0, value).astype(BF16)
+
+    loop(3, finish_input)
+    grad_copy = pltpu.make_async_copy(d_att, grad_input, local.at[18])
+    grad_copy.start()
+    close(4)
+    close(5)
+    vector_step(4)
+    out_vectors[...] = vec[5]
+    for u in (0, 1, 4, 5):
+        swap_copy(u).wait()
+        put_half(u, 1 - core, in5[u].astype(F32))
+    grad_copy.wait()
+
+
+def fused_layer(
+    hidden_in,
+    cotangent,
+    span_mask,
+    lengths,
+    repeats,
+    mask_embedding,
+    query_weight,
+    query_bias,
+    key_weight,
+    value_weight,
+    value_bias,
+    output_weight,
+    output_bias,
+    mixing_gain,
+    mixing_shift,
+    inner_weight,
+    inner_bias,
+    outer_weight,
+    outer_bias,
+    final_gain,
+    final_shift,
+):
+    params = jnp.concatenate(
+        [
+            v.astype(F32)
+            for v in (
+                mask_embedding,
+                query_bias,
+                value_bias,
+                output_bias,
+                mixing_gain,
+                mixing_shift,
+                inner_bias,
+                outer_bias,
+                final_gain,
+                final_shift,
+            )
+        ]
+    ).reshape(13, 768)
+    vmem = pl.BlockSpec(memory_space=pltpu.VMEM)
+    anywhere = pl.BlockSpec(memory_space=pl.ANY)
+    scalars = pl.BlockSpec(memory_space=pltpu.SMEM)
+    bf = lambda *shape: pltpu.VMEM(shape, BF16)
+    fl = lambda *shape: pltpu.VMEM(shape, F32)
+    dma = lambda *shape: pltpu.SemaphoreType.DMA(shape)
+    shape = lambda dims, dtype: jax.ShapeDtypeStruct(dims, dtype)
+    result = pl.pallas_call(
+        layer_body,
+        out_shape=[
+            shape((384, 768), BF16),
+            shape((384, 768), BF16),
+            shape((9216, 256), BF16),
+            shape((96, 192), F32),
+            shape((96, 192), F32),
+            shape((96, 192), F32),
+            shape((96, 192), F32),
+            shape((96, 768), F32),
+            shape((384, 192), F32),
+            shape((16, 768), F32),
+        ],
+        in_specs=[anywhere] * 8 + [vmem, vmem, scalars, scalars],
+        out_specs=[anywhere] * 3 + [vmem] * 7,
+        scratch_shapes=[
+            bf(3072, 768),
+            bf(3072, 768),
+            bf(768, 768),
+            bf(768, 768),
+            bf(768, 768),
+            bf(768, 768),
+            bf(3, 512, 768),
+            bf(3, 512, 768),
+            bf(3, 512, 768),
+            bf(384, 768),
+            bf(384, 768),
+            bf(9216, 256),
+            bf(384, 768),
+            fl(384, 768),
+            fl(384, 1),
+            fl(384, 768),
+            fl(384, 768),
+            bf(384, 768),
+            bf(384, 768),
+            pltpu.VMEM((4, 8, 128), jnp.int32),
+            fl(512, 8),
+            fl(12, 8, 256),
+            bf(6, 2, 2, 2, 2, 2, 96, 384),
+            bf(SLOTS, 2, 2, 2, 2, 96, 384),
+            bf(6, 2, 2, 2, 96, 384),
+            bf(6, 2, 2, 96, 384),
+            bf(6, 2, 96, 384),
+            bf(6, 96, 384),
+            bf(6, 96, 384),
+            bf(2, 384, 768),
+            bf(384, 768),
+            fl(6, 16, 768),
+            fl(5, 16, 768),
+            dma(6, 6),
+            dma(6, 6),
+            dma(4, 3),
+            dma(4, 3),
+            dma(3),
+            dma(3),
+            dma(5),
+            dma(5),
+            dma(19),
+            pltpu.SemaphoreType.REGULAR,
+        ],
+        compiler_params=pltpu.CompilerParams(
+            collective_id=1, has_side_effects=True, vmem_limit_bytes=63 * 2**20
+        ),
+        name="fused_layer",
+    )(
+        hidden_in,
+        cotangent.reshape(384, 768),
+        query_weight,
+        key_weight,
+        value_weight,
+        output_weight,
+        inner_weight,
+        outer_weight,
+        span_mask,
+        params,
+        lengths,
+        repeats,
+    )
+    layer_out, grad_input, _, g_query, g_key, g_value, g_output, g_inner, g_outer, vectors = result
+    return (
+        layer_out.reshape(3, 128, 768),
+        grad_input.reshape(3, 128, 768),
+        vectors[0],
+        g_query,
+        vectors[1],
+        g_key,
+        g_value,
+        vectors[2],
+        g_output,
+        vectors[3],
+        vectors[4],
+        vectors[5],
+        g_inner,
+        vectors[6:10].reshape(-1),
+        g_outer,
+        vectors[10],
+        vectors[11],
+        vectors[12],
+    )
 
 
 def with_halo(x, sides, width):
@@ -47,7 +931,7 @@
     return jax.nn.gelu(inputs, approximate=False)
 
 
-def shards(
+def plain_layer(
     hidden_in,
     cotangent,
     span_mask,
@@ -251,8 +1135,9 @@
 
 
 def solution(mesh):
+    fused = mesh.shape["batch"] == 8 and mesh.shape["seq"] == 4
     return jax.shard_map(
-        shards,
+        fused_layer if fused else plain_layer,
         mesh=mesh,
         in_specs=(
             P("batch", "seq", None),

time: 1020 us -> 188 us (0.18)
  waiting for transfers between devices: 705 us -> 0 us
  matrix products: 171 us -> 0 us
  Pallas kernels: 0 us -> 166 us
  blocking collectives: 41.1 us -> 0 us
  local copies, waits for them, and re-layouts: 58 us -> 20.1 us
  other arithmetic: 19.6 us -> 0.01 us
  between operations: 14.8 us -> 0.7 us
    reduce_scatter x9 -> x0, waiting for transfers between devices: 607 us -> none  [the longest x1 166 us: shards(): lax.psum_scatter(matrices[5], 'batch', scatter_dimension=0, tiled=True)]
    dot_general x24 -> x0, matrix products: 171 us -> none  [the longest x1 37.9 us: shards(): jnp.einsum('rhqk,rkhd->rqhd', d_raw, key_heads, preferred_element_type=jn...]
    pallas_call x0 -> x1, Pallas kernels: none -> 166 us  [fused_layer(): pl.pallas_call(layer_body, out_shape=[shape((384, 768), BF16), shape((384...]
    unnamed x21 -> x0, waiting for transfers between devices: 66.6 us -> none
    psum x1 -> x0, blocking collectives: 41.1 us -> none  [shards(): lax.psum((g_mask, g_query_bias, g_value_bias, g_output_bias, d_mixing_gai...]
    all_gather x2 -> x0, waiting for transfers between devices: 28.1 us -> none  [the longest x1 14.1 us: shards(): lax.all_gather(value_rows, 'seq', axis=1, tiled=True)]
    reshape x6 -> x2, local copies, waits for them, and re-layouts: 21.9 us -> 1.26 us  [the longest x1 0.66 us: fused_layer(): params = jnp.concatenate([v.astype(F32) for v in (mask_embedding, query_b...]
    unnamed x102 -> x29, local copies, waits for them, and re-layouts: 23.9 us -> 15.6 us
  transfers between devices with their start and end apart: 18 -> 0, of which waited for: 13 -> 0; matrix products, arithmetic and copies ran while one was open for 17% -> 0% of each run, Pallas kernels for 0% -> 0%
where the time goes in v2:
time: 188 us; the launch traced here: 187 us
  Pallas kernels  166 us (88%)
  local copies, waits for them, and re-layouts  20.1 us (11%)
    pallas_call x1, Pallas kernels, fused_layer(): pl.pallas_call(layer_body, out_shape=[shape((384, 768), BF16), shape((384...  166 us
    unnamed x29, local copies, waits for them, and re-layouts  15.6 us

profile of v2, /device:TPU:0, one launch (start us, length us, event | category | flops | bytes accessed | tf_op | source)
XLA Modules:
  0.0 186.9 jit_solution(15652663278326248739)
XLA Ops:
  0.7 0.9 dynamic-update-slice
  1.5 0.8 dynamic-update-slice.1
  2.4 0.9 dynamic-update-slice.2
  3.2 0.9 dynamic-update-slice.3
  4.1 0.9 dynamic-update-slice.4
  4.9 0.8 dynamic-update-slice.5
  5.8 0.9 dynamic-update-slice.6
  6.7 0.9 dynamic-update-slice.7
  7.5 0.9 dynamic-update-slice.8
  8.4 0.7 constant_dynamic-update-slice_fusion
  9.1 0.7 reshape.60.params
  9.7 166.1 %fused_layer.1 = (bf16[384,768]{1,0:T(8,128)(2,1)}, bf16[384,768]{1,0:T(8,128)(2,1)}, bf16[9216,256]{1,0:T(8,128)(2,1)}, f32[96,192]{1,0:T(8,128)}, f32[96,192]{...) custom-call(bf16[3,128,768]{2,1,0:T(8,128)(2,1)} %hidden.1, ...), custom_call_target="tpu_custom_call" | custom-call | tf_op jit(solution)/shard_map/fused_layer/pallas_call | solution.py:793
  175.9 0.9 slice.36
  176.7 1.7 slice_reduce_fusion
  178.4 0.6 reshape.58
  179.0 1.9 copy.39
  180.9 2.0 %copy.57 = bf16[3,128,768]{2,1,0:T(8,128)(2,1)} copy(bf16[3,128,768]{2,1,0:T(8,128)(2,1)} %bitcast.5) | data formatting | bytes 1179648
  182.8 0.8 copy.58
  183.7 0.6 copy.59
  184.3 0.6 copy.60
  184.9 0.6 copy.61
  185.6 0.0 copy-done.2
  185.6 0.6 copy.62
  186.2 0.7 copy.63
  (12 shorter events, 0.0 us)
Async XLA Ops:
  175.8 7.0 %copy-start = (bf16[384,768]{1,0:T(8,128)(2,1)S(1)}, bf16[384,768]{1,0:T(8,128)(2,1)}, u32[]{:S(2)}) copy-start(bf16[384,768]{1,0:T(8,128)(2,1)} %get-tuple-element.28) | copy-start | bytes 1769476
  180.9 2.8 %copy-start.5 = (f32[96,192]{1,0:T(8,128)S(1)}, f32[96,192]{1,0:T(8,128)}, u32[]{:S(2)}) copy-start(f32[96,192]{1,0:T(8,128)} %get-tuple-element.84) | copy-start | bytes 221188
  180.9 3.4 %copy-start.4 = (f32[96,192]{1,0:T(8,128)S(1)}, f32[96,192]{1,0:T(8,128)}, u32[]{:S(2)}) copy-start(f32[96,192]{1,0:T(8,128)} %get-tuple-element.86) | copy-start | bytes 221188
  180.9 4.1 %copy-start.3 = (f32[96,192]{1,0:T(8,128)S(1)}, f32[96,192]{1,0:T(8,128)}, u32[]{:S(2)}) copy-start(f32[96,192]{1,0:T(8,128)} %get-tuple-element.87) | copy-start | bytes 221188
  182.8 2.8 %copy-start.2 = (f32[96,192]{1,0:T(8,128)S(1)}, f32[96,192]{1,0:T(8,128)}, u32[]{:S(2)}) copy-start(f32[96,192]{1,0:T(8,128)} %get-tuple-element.89) | copy-start | bytes 221188
  182.8 3.4 %copy-start.1 = (f32[96,768]{1,0:T(8,128)S(1)}, f32[96,768]{1,0:T(8,128)}, u32[]{:S(2)}) copy-start(f32[96,768]{1,0:T(8,128)} %get-tuple-element.93) | copy-start | bytes 884740

commit v3 on v2

--- a/solution.py
+++ b/solution.py
@@ -61,72 +61,67 @@
 
 
 class Unit:
-    def __init__(self, number, order, both, inbox, sends, recvs, spot, peer):
-        self.number, self.order, self.both, self.inbox = number, order, both, inbox
+    def __init__(self, order, both, inbox, sends, recvs, spot, peer):
+        self.order, self.both, self.inbox = order, both, inbox
         self.sends, self.recvs, self.spot, self.peer = sends, recvs, spot, peer
         self.own = both.at[spot["core"]]
-
-    def axis(self, phase):
-        return ("core", *self.order, "zlo", "zhi")[phase]
+        self.phase = 0
 
     def where(self, phase, stays):
-        spot = self.spot
-        first = self.order[0]
-        here = lambda name: spot[name] if stays else 1 - spot[name]
-        if phase == 1 and first == "x":
-            return (slice(None), slice(None), slice(None), here("x"))
-        if phase == 1:
-            return (here("y"),)
-        if phase == 2 and first == "x":
-            return (here("y"), slice(None), slice(None), spot["x"])
-        if phase == 2:
-            return (spot["y"], slice(None), slice(None), here("x"))
-        if phase == 3:
-            return (spot["y"], slice(None), here("zlo"), spot["x"])
-        return (spot["y"], here("zhi"), spot["zlo"], spot["x"])
+        done, axis = self.order[: phase - 1], self.order[phase - 1]
+        place = []
+        for name in ("y", "zhi", "zlo", "x"):
+            side = self.spot[name]
+            if name == axis:
+                place.append(side if stays else 1 - side)
+            else:
+                place.append(side if name in done else slice(None))
+        return tuple(place)
 
     def copy(self, phase):
         if phase == 0:
-            source = self.both.at[1 - self.spot["core"]]
+            axis, source = "core", self.both.at[1 - self.spot["core"]]
         else:
-            source = self.own.at[self.where(phase, False)]
+            axis, source = self.order[phase - 1], self.own.at[self.where(phase, False)]
         return pltpu.make_async_remote_copy(
             src_ref=source,
             dst_ref=self.inbox[phase],
-            send_sem=self.sends.at[self.number, phase],
-            recv_sem=self.recvs.at[self.number, phase],
-            device_id=self.peer[self.axis(phase)],
+            send_sem=self.sends.at[phase],
+            recv_sem=self.recvs.at[phase],
+            device_id=self.peer[axis],
             device_id_type=MESH,
         )
 
-    def start(self, phase):
-        self.copy(phase).start()
-
-    def finish(self, phase):
+    def start(self):
+        self.copy(0).start()
+
+    def step(self):
+        phase = self.phase
         self.copy(phase).wait()
         came = self.inbox[phase]
         target = self.own if phase == 0 else self.own.at[self.where(phase, True)]
-        lead = came.shape[:-2]
-        count = 1
-        for size in lead:
-            count *= size
+        lead = 4 - phase
 
         def body(n):
-            place = []
-            for size in reversed(lead):
-                place.append(lax.rem(n, size))
-                n = n // size
-            place = tuple(reversed(place))
+            place = tuple(lax.rem(n // 2 ** (lead - 1 - i), 2) for i in range(lead))
             target[place] = target[place] + came[place]
 
-        loop(count, body)
-
-    def step(self, phase):
-        self.finish(phase)
-        self.start(phase + 1)
-
-
-ORDERS = (("x", "y"), ("y", "x"), ("x", "y"), ("y", "x"), ("x", "y"), ("y", "x"))
+        loop(2**lead, body)
+        self.phase = phase + 1
+        self.copy(self.phase).start()
+
+
+NAMES = ("outer0", "outer1", "inner0", "inner1", "output", "query", "key", "value")
+ORDERS = {
+    "outer0": ("x", "y", "zlo", "zhi"),
+    "outer1": ("y", "x", "zlo", "zhi"),
+    "inner0": ("x", "y", "zlo", "zhi"),
+    "inner1": ("zlo", "y", "x", "zhi"),
+    "output": ("y", "x", "zlo", "zhi"),
+    "query": ("x", "y", "zlo", "zhi"),
+    "key": ("x", "zlo", "zhi", "y"),
+    "value": ("zlo", "zhi", "x", "y"),
+}
 SLOTS = 3
 
 
@@ -140,7 +135,16 @@
     inner_weight,
     outer_weight,
     span,
-    params,
+    mask_embedding,
+    query_bias,
+    value_bias,
+    output_bias,
+    mixing_gain,
+    mixing_shift,
+    inner_bias,
+    outer_bias,
+    final_gain,
+    final_shift,
     lengths,
     repeats,
     layer_out,
@@ -159,6 +163,7 @@
     wk,
     wv,
     wo,
+    params,
     x_all,
     k_all,
     v_all,
@@ -175,13 +180,20 @@
     masks,
     wide,
     inner_sums,
-    grads,
+    mask_sums,
+    big_grads,
+    small_grads,
     in0,
-    in1,
-    in2,
-    in3,
-    in4,
-    in5,
+    big1,
+    big2,
+    big3,
+    big4,
+    big5,
+    small1,
+    small2,
+    small3,
+    small4,
+    small5,
     d_in0,
     d_in1,
     vec,
@@ -226,6 +238,12 @@
         pl.semaphore_signal(barrier, inc=1, device_id=peer[name], device_id_type=MESH)
     pl.semaphore_wait(barrier, len(names))
 
+    vectors = [mask_embedding, query_bias, value_bias, output_bias, mixing_gain, mixing_shift]
+    vectors += [inner_bias.at[pl.ds(768 * i, 768)] for i in range(4)]
+    vectors += [outer_bias, final_gain, final_shift]
+    for i, vector in enumerate(vectors):
+        params[i : i + 1] = vector[...].astype(F32).reshape(1, 768)
+
     masks[me] = jnp.zeros((8, 128), jnp.int32)
     masks[me, 0:3] = span[...]
     mask_copies = []
@@ -417,13 +435,24 @@
     )
     out_copy.start()
 
-    units = []
-    for u in range(6):
-        inbox = [in0.at[u % SLOTS], in1.at[u], in2.at[u], in3.at[u], in4.at[u]]
-        units.append(Unit(u, ORDERS[u], grads.at[u], inbox, sends, recvs, spot, peer))
-
-    def free_slot():
-        pl.semaphore_signal(credit, inc=1, device_id=peer["core"], device_id_type=MESH)
+    units = {}
+    for u, name in enumerate(NAMES):
+        if u < 4:
+            both = big_grads.at[u]
+            inbox = [in0.at[u % SLOTS], big1.at[u], big2.at[u], big3.at[u], big4.at[u]]
+        else:
+            n = u - 4
+            both = small_grads.at[n]
+            first = in0.at[1 + n // 2, :, :, :, :, pl.ds(48 * (n % 2), 48)]
+            inbox = [first, small1.at[n], small2.at[n], small3.at[n], small4.at[n]]
+        units[name] = Unit(ORDERS[name], both, inbox, sends.at[u], recvs.at[u], spot, peer)
+
+    def step(*which):
+        for name in which:
+            units[name].step()
+
+    def free_slot(count):
+        pl.semaphore_signal(credit, inc=count, device_id=peer["core"], device_id_type=MESH)
 
     def claim_slot():
         pl.semaphore_wait(credit, 1)
@@ -437,13 +466,13 @@
                 for i in range(2):
                     for side in range(2):
                         rows = (h * 2 + i) * 96
-                        grads[i, h, side, z // 2, lax.rem(z, 2), x] = grad[
+                        big_grads[i, h, side, z // 2, lax.rem(z, 2), x] = grad[
                             rows : rows + 96, side * 384 : side * 384 + 384
                         ]
 
     loop(4, outer_grads)
-    units[0].start(0)
-    units[1].start(0)
+    units["outer0"].start()
+    units["outer1"].start()
 
     def d_hidden_units(j):
         d_act = mm_t(d_outer[...], wf[aligned(j, 256)])
@@ -453,26 +482,24 @@
         inner_sums[j] = fold(low.astype(F32))
 
     loop(12, d_hidden_units)
+    step("outer0")
+    free_slot(1)
+    step("outer1")
+    free_slot(2)
 
     def inner_grads(s):
         cols = [region[pl.ds(pl.multiple_of((12 + 3 * s + j) * 384, 384), 384)] for j in range(3)]
         grad = mm_tl(first_low[...], jnp.concatenate(cols, axis=1)).astype(BF16)
         for b in range(8):
             for i in range(2):
-                grads[2 + i, lax.rem(s, 2), s // 2, b // 4, (b // 2) % 2, b % 2] = grad[
+                big_grads[2 + i, lax.rem(s, 2), s // 2, b // 4, (b // 2) % 2, b % 2] = grad[
                     96 * b : 96 * b + 96, 384 * i : 384 * i + 384
                 ]
 
     loop(4, inner_grads)
-    units[2].start(0)
-    for u in range(2):
-        units[u].step(0)
-        if u == 0:
-            free_slot()
-            claim_slot()
-            units[3].start(0)
-        else:
-            free_slot()
+    units["inner0"].start()
+    claim_slot()
+    units["inner1"].start()
 
     def d_first_part(n):
         cols = aligned(n, 256)
@@ -520,27 +547,31 @@
     put_sum(5, sums[1])
     put_sum(3, sums[2])
 
-    def square_grads(u, lower, left, right):
+    def square_grads(name, left, right):
+        u = NAMES.index(name) - 4
         for m in range(2):
             grad = mm_tl(left(m), right).astype(BF16)
             for b in range(4):
                 for h in range(2):
                     for side in range(2):
                         rows = b * 96 + h * 48
-                        grads[u, h, side, m, b // 2, b % 2, pl.ds(lower * 48, 48)] = grad[
+                        small_grads[u, h, side, m, b // 2, b % 2] = grad[
                             rows : rows + 48, side * 384 : side * 384 + 384
                         ]
-
-    square_grads(4, 0, lambda m: mixed[:, 384 * m : 384 * m + 384], d_att[...])
+        claim_slot()
+        units[name].start()
+
+    step("inner0")
+    free_slot(2)
+    step("inner1")
+    square_grads("output", lambda m: mixed[:, 384 * m : 384 * m + 384], d_att[...])
 
     def d_mixed_part(i):
         rows = aligned(i, 128)
         mixed[rows] = mm_t(d_att[rows], wo[...]).astype(BF16)
 
     loop(3, d_mixed_part)
-    units[2].step(0)
-    free_slot()
-    units[3].step(0)
+    step("outer0", "outer1")
 
     for r in range(3):
         refills[r].wait()
@@ -565,14 +596,11 @@
 
         loop(6, attend_back)
         if r == 0:
-            units[0].step(1)
-            units[1].step(1)
+            step("output")
         elif r == 1:
-            units[0].step(2)
-            units[1].step(2)
+            step("inner1")
         else:
-            units[2].step(1)
-            units[3].step(1)
+            step("outer0", "outer1", "output")
 
     def own_inputs(m):
         return jnp.concatenate(
@@ -582,34 +610,36 @@
     def all_inputs(m):
         return jnp.concatenate([x_all[r, :, pl.ds(384 * m, 384)] for r in range(3)], 0)
 
-    square_grads(4, 1, own_inputs, q_own[...])
-    claim_slot()
-    units[4].start(0)
-    square_grads(5, 0, all_inputs, wi[pl.ds(0, 1536)])
-    square_grads(5, 1, all_inputs, wi[pl.ds(1536, 1536)])
-    claim_slot()
-    units[5].start(0)
+    square_grads("query", own_inputs, q_own[...])
+    square_grads("key", all_inputs, wi[pl.ds(0, 1536)])
+    step("inner0", "query")
+    square_grads("value", all_inputs, wi[pl.ds(1536, 1536)])
+    step("outer0", "outer1", "inner1", "key")
     put_sum(1, fold(q_own[...].astype(F32)))
 
     def value_sum(i, acc):
         return acc + fold(wi[pl.ds(pl.multiple_of(1536 + i * 128, 128), 128)].astype(F32))
 
     put_sum(2, lax.fori_loop(0, 12, value_sum, nothing))
-    units[0].step(3)
-    units[1].step(3)
-
-    mask_sum = nothing
+    mask_sums[...] = jnp.zeros((3, 8, 256), F32)
     for r in range(3):
 
-        def d_in_part(s, acc):
-            part = mm_t(wi[pl.ds(pl.multiple_of(512 * r + s * 128, 128), 128)], wk[...]) + mm_t(
-                wi[pl.ds(pl.multiple_of(1536 + 512 * r + s * 128, 128), 128)], wv[...]
+        def d_in_part(n, carry):
+            cols = aligned(n, 256)
+            part = mm_t(wi[pl.ds(512 * r, 512)], wk[cols]) + mm_t(
+                wi[pl.ds(1536 + 512 * r, 512)], wv[cols]
             )
-            chosen = wide[aligned(s, 128), r : r + 1]
-            wf[pl.ds(pl.multiple_of(s * 384 + r * 128, 128), 128)] = part.astype(BF16)
-            return acc + fold(part * chosen)
-
-        mask_sum = lax.fori_loop(0, 4, d_in_part, mask_sum)
+            for s in range(4):
+                piece = part[128 * s : 128 * s + 128]
+                wf[pl.ds(s * 384 + r * 128, 128), cols] = piece.astype(BF16)
+            mask_sums[n] = mask_sums[n] + fold(part * wide[:, r : r + 1])
+            return carry
+
+        lax.fori_loop(0, 3, d_in_part, 0)
+        if r == 0:
+            step("value")
+        elif r == 1:
+            step("output")
 
     def d_in_copy(i):
         if i < 2:
@@ -636,6 +666,7 @@
         chosen = jnp.where(i == 0, chosen[:, 0:1], jnp.where(i == 1, chosen[:, 1:2], chosen[:, 2:3]))
         return acc + fold(part * chosen)
 
+    mask_sum = jnp.concatenate([mask_sums[n] for n in range(3)], axis=1)
     put_sum(0, lax.fori_loop(0, 3, own_part, mask_sum))
 
     def vector_copy(phase):
@@ -664,40 +695,30 @@
 
     loop(3, add_across)
     d_in_copy(2).start()
-    units[4].step(0)
-    units[5].step(0)
+    step("inner0")
     vector_step(0)
-    units[2].step(2)
-    units[3].step(2)
+    step("query", "key")
     vector_step(1)
-    units[4].step(1)
-    units[5].step(1)
-    vector_step(2)
-    units[2].step(3)
-    units[3].step(3)
-    units[4].step(2)
-    units[5].step(2)
-    vector_step(3)
-
     mine = (y, spot["zhi"], spot["zlo"], spot["x"])
 
     def swap_copy(u):
         return pltpu.make_async_remote_copy(
-            src_ref=units[u].own.at[mine],
-            dst_ref=in5.at[u],
+            src_ref=units[NAMES[u]].own.at[mine],
+            dst_ref=big5.at[u] if u < 2 else small5.at[u - 4],
             send_sem=sends.at[u, 5],
             recv_sem=recvs.at[u, 5],
             device_id=peer["core"],
             device_id_type=MESH,
         )
 
-    def close(u):
-        units[u].copy(4).wait()
-        result = units[u].own[mine].astype(F32) + in4[u].astype(F32)
+    def close(name):
+        u, unit = NAMES.index(name), units[name]
+        unit.copy(4).wait()
+        result = unit.own[mine].astype(F32) + unit.inbox[4][...].astype(F32)
         if u == 2 or u == 3:
             out_inner[:, pl.ds(384 * (u - 2), 384)] = result
             return
-        units[u].own[mine] = result.astype(BF16)
+        unit.own[mine] = result.astype(BF16)
         swap_copy(u).start()
         put_half(u, core, result)
 
@@ -705,15 +726,30 @@
         value = jnp.where(core == 0, value[:, :192], pltpu.roll(value, 192, 1)[:, :192])
         if u < 2:
             out_outer[pl.ds(pl.multiple_of(side * 192 + u * 96, 96), 96)] = value
-            return
-        targets = (out_output, out_query) if u == 4 else (out_key, out_value)
-        for i, target in enumerate(targets):
-            target[pl.ds(pl.multiple_of(side * 48, 48), 48)] = value[48 * i : 48 * i + 48]
-
-    for u in range(4):
-        close(u)
-    units[4].step(3)
-    units[5].step(3)
+        else:
+            target = (out_output, out_query, out_key, out_value)[u - 4]
+            target[pl.ds(pl.multiple_of(side * 48, 48), 48)] = value
+
+    def open_half(name):
+        u = NAMES.index(name)
+        swap_copy(u).wait()
+        put_half(u, 1 - core, (big5[u] if u < 2 else small5[u - 4]).astype(F32))
+
+    close("outer0")
+    close("outer1")
+    step("output", "value")
+    vector_step(2)
+    step("query", "key")
+    vector_step(3)
+    step("inner0", "inner1")
+    open_half("outer0")
+    open_half("outer1")
+    close("output")
+    step("value", "query", "key")
+    vector_step(4)
+    open_half("output")
+    close("inner0")
+    close("inner1")
 
     d_in_copy(2).wait()
 
@@ -733,14 +769,26 @@
     loop(3, finish_input)
     grad_copy = pltpu.make_async_copy(d_att, grad_input, local.at[18])
     grad_copy.start()
-    close(4)
-    close(5)
-    vector_step(4)
     out_vectors[...] = vec[5]
-    for u in (0, 1, 4, 5):
-        swap_copy(u).wait()
-        put_half(u, 1 - core, in5[u].astype(F32))
+    step("value")
+    close("query")
+    close("key")
+    close("value")
+    open_half("query")
+    open_half("key")
+    open_half("value")
     grad_copy.wait()
+
+
+def hand_out(*refs):
+    sources, vectors, targets, rows = refs[:8], refs[8], refs[9:17], refs[17:27]
+    for source, target in zip(sources, targets):
+        target[...] = source[...]
+    for i, place in enumerate((0, 1, 2, 3, 4, 5, None, 10, 11, 12)):
+        if place is not None:
+            rows[i][...] = vectors[place]
+    for j in range(4):
+        rows[6][pl.ds(768 * j, 768)] = vectors[6 + j]
 
 
 def fused_layer(
@@ -766,23 +814,6 @@
     final_gain,
     final_shift,
 ):
-    params = jnp.concatenate(
-        [
-            v.astype(F32)
-            for v in (
-                mask_embedding,
-                query_bias,
-                value_bias,
-                output_bias,
-                mixing_gain,
-                mixing_shift,
-                inner_bias,
-                outer_bias,
-                final_gain,
-                final_shift,
-            )
-        ]
-    ).reshape(13, 768)
     vmem = pl.BlockSpec(memory_space=pltpu.VMEM)
     anywhere = pl.BlockSpec(memory_space=pl.ANY)
     scalars = pl.BlockSpec(memory_space=pltpu.SMEM)
@@ -804,7 +835,7 @@
             shape((384, 192), F32),
             shape((16, 768), F32),
         ],
-        in_specs=[anywhere] * 8 + [vmem, vmem, scalars, scalars],
+        in_specs=[anywhere] * 8 + [vmem] * 11 + [scalars, scalars],
         out_specs=[anywhere] * 3 + [vmem] * 7,
         scratch_shapes=[
             bf(3072, 768),
@@ -813,6 +844,7 @@
             bf(768, 768),
             bf(768, 768),
             bf(768, 768),
+            fl(16, 768),
             bf(3, 512, 768),
             bf(3, 512, 768),
             bf(3, 512, 768),
@@ -829,19 +861,26 @@
             pltpu.VMEM((4, 8, 128), jnp.int32),
             fl(512, 8),
             fl(12, 8, 256),
-            bf(6, 2, 2, 2, 2, 2, 96, 384),
+            fl(3, 8, 256),
+            bf(4, 2, 2, 2, 2, 2, 96, 384),
+            bf(4, 2, 2, 2, 2, 2, 48, 384),
             bf(SLOTS, 2, 2, 2, 2, 96, 384),
-            bf(6, 2, 2, 2, 96, 384),
-            bf(6, 2, 2, 96, 384),
-            bf(6, 2, 96, 384),
-            bf(6, 96, 384),
-            bf(6, 96, 384),
+            bf(4, 2, 2, 2, 96, 384),
+            bf(4, 2, 2, 96, 384),
+            bf(4, 2, 96, 384),
+            bf(4, 96, 384),
+            bf(2, 96, 384),
+            bf(4, 2, 2, 2, 48, 384),
+            bf(4, 2, 2, 48, 384),
+            bf(4, 2, 48, 384),
+            bf(4, 48, 384),
+            bf(4, 48, 384),
             bf(2, 384, 768),
             bf(384, 768),
             fl(6, 16, 768),
             fl(5, 16, 768),
-            dma(6, 6),
-            dma(6, 6),
+            dma(8, 6),
+            dma(8, 6),
             dma(4, 3),
             dma(4, 3),
             dma(3),
@@ -865,30 +904,50 @@
         inner_weight,
         outer_weight,
         span_mask,
-        params,
+        mask_embedding,
+        query_bias,
+        value_bias,
+        output_bias,
+        mixing_gain,
+        mixing_shift,
+        inner_bias,
+        outer_bias,
+        final_gain,
+        final_shift,
         lengths,
         repeats,
     )
-    layer_out, grad_input, _, g_query, g_key, g_value, g_output, g_inner, g_outer, vectors = result
+    arrays, vectors = [result[0], result[1], *result[3:9]], result[9]
+    wide_row = shape((768,), F32)
+    handed = pl.pallas_call(
+        hand_out,
+        out_shape=[shape(v.shape, v.dtype) for v in arrays]
+        + [wide_row] * 6
+        + [shape((3072,), F32)]
+        + [wide_row] * 3,
+        in_specs=[vmem] * 9,
+        out_specs=[vmem] * 18,
+        name="hand_out",
+    )(*arrays, vectors)
+    layer_out, grad_input, g_query, g_key, g_value, g_output, g_inner, g_outer = handed[:8]
+    g_mask, g_q_bias, g_v_bias, g_o_bias, g_gain, g_shift, g_inner_bias, *g_last = handed[8:]
     return (
         layer_out.reshape(3, 128, 768),
         grad_input.reshape(3, 128, 768),
-        vectors[0],
+        g_mask,
         g_query,
-        vectors[1],
+        g_q_bias,
         g_key,
         g_value,
-        vectors[2],
+        g_v_bias,
         g_output,
-        vectors[3],
-        vectors[4],
-        vectors[5],
+        g_o_bias,
+        g_gain,
+        g_shift,
         g_inner,
-        vectors[6:10].reshape(-1),
+        g_inner_bias,
         g_outer,
-        vectors[10],
-        vectors[11],
-        vectors[12],
+        *g_last,
     )
 
 

time: 188 us -> 150 us (0.80)
  Pallas kernels: 166 us -> 147 us
  local copies, waits for them, and re-layouts: 20.1 us -> 1.86 us
    pallas_call x1, Pallas kernels: 166 us -> 144 us  [fused_layer(): pl.pallas_call(layer_body, out_shape=[shape((384, 768), BF16), shape((384...]
    unnamed x29 -> x1, local copies, waits for them, and re-layouts: 15.6 us -> 1.86 us
    pallas_call x0 -> x1, Pallas kernels: none -> 3 us  [fused_layer(): pl.pallas_call(hand_out, out_shape=[shape(v.shape, v.dtype) for v in arra...]
    slice x2 -> x0, local copies, waits for them, and re-layouts: 2.54 us -> none  [the longest x1 1.67 us: fused_layer(): vectors[12]]
where the time goes in v3:
time: 150 us
  Pallas kernels  147 us (98%)
  local copies, waits for them, and re-layouts  1.86 us (1%)
    pallas_call x1, Pallas kernels, fused_layer(): pl.pallas_call(layer_body, out_shape=[shape((384, 768), BF16), shape((384...  144 us
    pallas_call x1, Pallas kernels, fused_layer(): pl.pallas_call(hand_out, out_shape=[shape(v.shape, v.dtype) for v in arra...  3 us

profile of v3, /device:TPU:0, one launch (start us, length us, event | category | flops | bytes accessed | tf_op | source)
XLA Modules:
  0.0 150.0 jit_solution(1563896475726657290)
XLA Ops:
  0.7 144.4 %fused_layer.1 = (bf16[384,768]{1,0:T(8,128)(2,1)}, bf16[384,768]{1,0:T(8,128)(2,1)}, bf16[9216,256]{1,0:T(8,128)(2,1)}, f32[96,192]{1,0:T(8,128)}, f32[96,192]{...) custom-call(bf16[3,128,768]{2,1,0:T(8,128)(2,1)} %hidden.1, ...), custom_call_target="tpu_custom_call" | custom-call | tf_op jit(solution)/shard_map/fused_layer/pallas_call | solution.py:824
  145.1 3.0 %hand_out.1 = (bf16[384,768]{1,0:T(8,128)(2,1)}, bf16[384,768]{1,0:T(8,128)(2,1)}, f32[96,192]{1,0:T(8,128)}, f32[96,192]{1,0:T(8,128)}, f32[96,192]{1,0:T(8,128...) custom-call(bf16[384,768]{1,0:T(8,128)(2,1)} %get-tuple-element.45.r, ...), custom_call_target="tpu_custom_call" | custom-call | tf_op jit(solution)/shard_map/hand_out/pallas_call | solution.py:922
  148.1 1.9 %copy.39 = f32[384,192]{0,1:T(8,128)} copy(f32[384,192]{1,0:T(8,128)} %get-tuple-element.86) | data formatting | bytes 589824

commit v4 on v3

--- a/solution.py
+++ b/solution.py
@@ -38,6 +38,14 @@
         return carry
 
     lax.fori_loop(0, count, step, 0)
+
+
+def span_loop(first, last, body):
+    def step(i, carry):
+        body(i)
+        return carry
+
+    lax.fori_loop(first, last, step, 0)
 
 
 def aligned(i, size):
@@ -111,18 +119,41 @@
         self.copy(self.phase).start()
 
 
-NAMES = ("outer0", "outer1", "inner0", "inner1", "output", "query", "key", "value")
+STARTS = (
+    "outer0", "outer1", "outer2", "outer3", "inner0", "inner1",
+    "inner2", "inner3", "output", "key", "query", "value",
+)
 ORDERS = {
-    "outer0": ("x", "y", "zlo", "zhi"),
-    "outer1": ("y", "x", "zlo", "zhi"),
-    "inner0": ("x", "y", "zlo", "zhi"),
+    "outer0": ("y", "zlo", "x", "zhi"),
+    "outer1": ("zlo", "x", "y", "zhi"),
+    "outer2": ("x", "zlo", "y", "zhi"),
+    "outer3": ("zlo", "y", "x", "zhi"),
+    "inner0": ("y", "zlo", "x", "zhi"),
     "inner1": ("zlo", "y", "x", "zhi"),
-    "output": ("y", "x", "zlo", "zhi"),
-    "query": ("x", "y", "zlo", "zhi"),
-    "key": ("x", "zlo", "zhi", "y"),
-    "value": ("zlo", "zhi", "x", "y"),
+    "inner2": ("y", "x", "zlo", "zhi"),
+    "inner3": ("x", "zlo", "y", "zhi"),
+    "output": ("x", "y", "zlo", "zhi"),
+    "key": ("y", "x", "zlo", "zhi"),
+    "query": ("x", "zlo", "zhi", "y"),
+    "value": ("x", "zlo", "y", "zhi"),
 }
-SLOTS = 3
+PLAN = (
+    "d_hidden", "outer0", "outer1", "outer2", "inner", "outer3", "d_first", "refill",
+    "fnb", "inner0", "inner1", "outer1", "outer0", "inner2", "outer2", "V1",
+    "dWo", "inner3", "W1", "dmixed", "ab00", "output", "outer1", "inner0",
+    "outer3", "ab01", "ab10", "inner1", "inner3", "W1", "ab11", "outer0",
+    "inner2", "ab20", "outer1", "ab21", "output", "outer2", "outer3", "dWk",
+    "outer0", "inner0", "inner1", "W1", "dWq", "inner2", "inner3", "dWv",
+    "key", "outer1", "query", "W1", "output", "inner0", "outer0", "outer2",
+    "inner1", "outer3", "outer1", "inner2", "inner3", "din0", "outer0", "din1",
+    "value", "W1", "output", "dc0", "din2", "inner0", "key", "outer2",
+    "dc1", "query", "vec", "inner1", "outer2", "outer3", "dc2", "W2",
+    "outer3", "inner2", "dy0", "inner3", "output", "value", "output", "query",
+    "dy1", "key", "W2", "value", "dy2", "W2", "query", "value",
+    "key", "W2", "query", "query", "value", "key", "value", "W2",
+    "key",
+)
+SLOTS = 6
 
 
 def layer_body(
@@ -181,23 +212,19 @@
     wide,
     inner_sums,
     mask_sums,
-    big_grads,
-    small_grads,
+    grads,
     in0,
-    big1,
-    big2,
-    big3,
-    big4,
-    big5,
-    small1,
-    small2,
-    small3,
-    small4,
-    small5,
+    in1,
+    in2,
+    in3,
+    in4,
+    in5,
     d_in0,
     d_in1,
     vec,
     vec_came,
+    late,
+    late_came,
     sends,
     recvs,
     x_send,
@@ -287,10 +314,6 @@
         )
     wide[...] = window.T
 
-    weight_loads["hidden"].wait()
-    weight_loads["key"].wait()
-    weight_loads["value"].wait()
-    weight_loads["query"].wait()
     half = lax.broadcasted_iota(jnp.int32, (128, 128), 1) < HEAD_DIM
     zero = jnp.zeros((128, 128), BF16)
 
@@ -302,33 +325,45 @@
 
     mask_row = params[0:1]
     spills = []
+
+    def put_mask(r, slot):
+        rows = aligned(slot, 128)
+        chosen = wide[rows, r : r + 1] > 0.5
+        kept = x_all[r, rows].astype(F32)
+        x_all[r, rows] = jnp.where(chosen, mask_row, kept).astype(BF16)
+
+    def project(pieces, with_queries):
+        inputs = jnp.concatenate([x_all[r, aligned(slot, 128)] for r, slot in pieces], 0)
+
+        def part(n):
+            cols = aligned(n, 256)
+            keys = mm(inputs, wk[:, cols]).astype(BF16)
+            values = (mm(inputs, wv[:, cols]) + params[2:3, cols]).astype(BF16)
+            for i, (r, slot) in enumerate(pieces):
+                k_all[r, aligned(slot, 128), cols] = keys[128 * i : 128 * i + 128]
+                v_all[r, aligned(slot, 128), cols] = values[128 * i : 128 * i + 128]
+            if with_queries:
+                q_own[:, cols] = (mm(inputs, wq[:, cols]) + params[1:2, cols]).astype(BF16)
+
+        loop(3, part)
+
+    weight_loads["hidden"].wait()
     for r in range(3):
-        x_copy(0, r).wait_recv()
-        x_copy(2, r).start()
-        x_copy(1, r).wait_recv()
+        put_mask(r, me)
+    for name in ("key", "value", "query"):
+        weight_loads[name].wait()
+    project([(r, me) for r in range(3)], True)
+    for r in range(3):
+        x_copy(1, r).wait()
+        put_mask(r, sibling)
+    project([(r, sibling) for r in range(3)], False)
+    x_copy(0, 0).wait_recv()
+    x_copy(2, 0).start()
+    for r in range(3):
         x_copy(2, r).wait()
-        x_copy(0, r).wait_send()
-        x_copy(1, r).wait_send()
-
-        def put_mask(i):
-            rows = aligned(i, 128)
-            chosen = wide[rows, r : r + 1] > 0.5
-            kept = x_all[r, rows].astype(F32)
-            x_all[r, rows] = jnp.where(chosen, mask_row, kept).astype(BF16)
-
-        loop(4, put_mask)
-
-        def project(n):
-            cols = aligned(n, 256)
-            x_row = x_all[r]
-            k_all[r, :, cols] = mm(x_row, wk[:, cols]).astype(BF16)
-            v_all[r, :, cols] = (mm(x_row, wv[:, cols]) + params[2:3, cols]).astype(BF16)
-            x_own = x_all[r, aligned(me, 128)]
-            q_own[pl.ds(128 * r, 128), cols] = (
-                mm(x_own, wq[:, cols]) + params[1:2, cols]
-            ).astype(BF16)
-
-        loop(3, project)
+        put_mask(r, across)
+        put_mask(r, 3 - me)
+        project([(r, across), (r, 3 - me)], False)
         key_live = lax.broadcasted_iota(jnp.int32, (1, 512), 1) < lengths[r]
 
         def attend(p):
@@ -344,12 +379,18 @@
             out = mm(probs, v_all[r, :, cols])
             mixed[pl.ds(128 * r, 128), cols] = unstacked(out).astype(BF16)
 
-        loop(6, attend)
+        span_loop(0, 3, attend)
+        if r < 2:
+            x_copy(0, r + 1).wait_recv()
+            x_copy(2, r + 1).start()
+        span_loop(3, 6, attend)
         rows = pl.ds(3072 * r, 3072)
         spill = pltpu.make_async_copy(region.at[rows], probs_out.at[rows], local.at[11 + r])
         spill.start()
         spills.append(spill)
 
+    for r in range(3):
+        x_copy(0, r).wait_send()
     weight_loads["output"].wait()
 
     def first_norm(i):
@@ -436,23 +477,17 @@
     out_copy.start()
 
     units = {}
-    for u, name in enumerate(NAMES):
-        if u < 4:
-            both = big_grads.at[u]
-            inbox = [in0.at[u % SLOTS], big1.at[u], big2.at[u], big3.at[u], big4.at[u]]
-        else:
-            n = u - 4
-            both = small_grads.at[n]
-            first = in0.at[1 + n // 2, :, :, :, :, pl.ds(48 * (n % 2), 48)]
-            inbox = [first, small1.at[n], small2.at[n], small3.at[n], small4.at[n]]
-        units[name] = Unit(ORDERS[name], both, inbox, sends.at[u], recvs.at[u], spot, peer)
-
-    def step(*which):
-        for name in which:
-            units[name].step()
-
-    def free_slot(count):
-        pl.semaphore_signal(credit, inc=count, device_id=peer["core"], device_id_type=MESH)
+    for u, name in enumerate(STARTS):
+        inbox = [in0.at[u % SLOTS], in1.at[u], in2.at[u], in3.at[u], in4.at[u]]
+        units[name] = Unit(ORDERS[name], grads.at[u], inbox, sends.at[u], recvs.at[u], spot, peer)
+
+    def start_unit(name):
+        if STARTS.index(name) >= SLOTS:
+            claim_slot()
+        units[name].start()
+
+    def free_slot():
+        pl.semaphore_signal(credit, inc=1, device_id=peer["core"], device_id_type=MESH)
 
     def claim_slot():
         pl.semaphore_wait(credit, 1)
@@ -463,16 +498,16 @@
             part = jnp.concatenate(cols, axis=1)[:, 384 * x : 384 * x + 384]
             grad = mm_tl(part, d_outer[...]).astype(BF16)
             for h in range(2):
-                for i in range(2):
+                for i in range(4):
                     for side in range(2):
-                        rows = (h * 2 + i) * 96
-                        big_grads[i, h, side, z // 2, lax.rem(z, 2), x] = grad[
-                            rows : rows + 96, side * 384 : side * 384 + 384
+                        rows = (h * 4 + i) * 48
+                        grads[STARTS.index(f"outer{i}"), h, side, z // 2, lax.rem(z, 2), x] = grad[
+                            rows : rows + 48, side * 384 : side * 384 + 384
                         ]
 
     loop(4, outer_grads)
-    units["outer0"].start()
-    units["outer1"].start()
+    for i in range(4):
+        start_unit(f"outer{i}")
 
     def d_hidden_units(j):
         d_act = mm_t(d_outer[...], wf[aligned(j, 256)])
@@ -481,25 +516,20 @@
         region[place] = low
         inner_sums[j] = fold(low.astype(F32))
 
-    loop(12, d_hidden_units)
-    step("outer0")
-    free_slot(1)
-    step("outer1")
-    free_slot(2)
-
     def inner_grads(s):
         cols = [region[pl.ds(pl.multiple_of((12 + 3 * s + j) * 384, 384), 384)] for j in range(3)]
         grad = mm_tl(first_low[...], jnp.concatenate(cols, axis=1)).astype(BF16)
         for b in range(8):
-            for i in range(2):
-                big_grads[2 + i, lax.rem(s, 2), s // 2, b // 4, (b // 2) % 2, b % 2] = grad[
-                    96 * b : 96 * b + 96, 384 * i : 384 * i + 384
-                ]
-
-    loop(4, inner_grads)
-    units["inner0"].start()
-    claim_slot()
-    units["inner1"].start()
+            for i in range(4):
+                rows, side = 96 * b + 48 * (i % 2), 384 * (i // 2)
+                grads[
+                    STARTS.index(f"inner{i}"), lax.rem(s, 2), s // 2, b // 4, (b // 2) % 2, b % 2
+                ] = grad[rows : rows + 48, side : side + 384]
+
+    def do_inner_grads():
+        loop(4, inner_grads)
+        for i in range(4):
+            start_unit(f"inner{i}")
 
     def d_first_part(n):
         cols = aligned(n, 256)
@@ -510,18 +540,21 @@
             acc = term if acc is None else acc + term
         total[:, cols] = acc
 
-    loop(3, d_first_part)
-    for j in range(12):
-        vec[0, 6 + j // 3 : 7 + j // 3, (j % 3) * 256 : (j % 3) * 256 + 256] = jnp.sum(
-            inner_sums[j], 0, keepdims=True
-        )
     refills = []
-    for r in range(3):
-        rows = pl.ds(3072 * r, 3072)
-        refill = pltpu.make_async_copy(probs_out.at[rows], region.at[rows], local.at[15 + r])
-        refill.start()
-        refills.append(refill)
-    out_copy.wait()
+
+    def do_d_first():
+        loop(3, d_first_part)
+        for j in range(12):
+            vec[0, 6 + j // 3 : 7 + j // 3, (j % 3) * 256 : (j % 3) * 256 + 256] = jnp.sum(
+                inner_sums[j], 0, keepdims=True
+            )
+
+    def refill_probs():
+        for r in range(3):
+            rows = pl.ds(3072 * r, 3072)
+            refill = pltpu.make_async_copy(probs_out.at[rows], region.at[rows], local.at[15 + r])
+            refill.start()
+            refills.append(refill)
 
     def first_norm_back(i, sums):
         rows = aligned(i, 64)
@@ -542,39 +575,36 @@
             sums[2] + fold(low.astype(F32)),
         )
 
-    sums = lax.fori_loop(0, 6, first_norm_back, (nothing, nothing, nothing))
-    put_sum(4, sums[0])
-    put_sum(5, sums[1])
-    put_sum(3, sums[2])
+    def do_first_norm_back():
+        out_copy.wait()
+        sums = lax.fori_loop(0, 6, first_norm_back, (nothing, nothing, nothing))
+        put_sum(4, sums[0])
+        put_sum(5, sums[1])
+        put_sum(3, sums[2])
 
     def square_grads(name, left, right):
-        u = NAMES.index(name) - 4
+        u = STARTS.index(name)
         for m in range(2):
             grad = mm_tl(left(m), right).astype(BF16)
             for b in range(4):
                 for h in range(2):
                     for side in range(2):
                         rows = b * 96 + h * 48
-                        small_grads[u, h, side, m, b // 2, b % 2] = grad[
+                        grads[u, h, side, m, b // 2, b % 2] = grad[
                             rows : rows + 48, side * 384 : side * 384 + 384
                         ]
-        claim_slot()
-        units[name].start()
-
-    step("inner0")
-    free_slot(2)
-    step("inner1")
-    square_grads("output", lambda m: mixed[:, 384 * m : 384 * m + 384], d_att[...])
+        start_unit(name)
+
+    def do_output_grads():
+        square_grads("output", lambda m: mixed[:, 384 * m : 384 * m + 384], d_att[...])
 
     def d_mixed_part(i):
         rows = aligned(i, 128)
         mixed[rows] = mm_t(d_att[rows], wo[...]).astype(BF16)
 
-    loop(3, d_mixed_part)
-    step("outer0", "outer1")
-
-    for r in range(3):
-        refills[r].wait()
+    def do_attend_back(r, first, last):
+        if first == 0:
+            refills[r].wait()
 
         def attend_back(p):
             cols = aligned(p, 128)
@@ -594,13 +624,7 @@
             wi[pl.ds(512 * r, 512), cols] = mm_tl(d_raw, queries).astype(BF16)
             wi[pl.ds(1536 + 512 * r, 512), cols] = mm_tl(low_probs, d_mix).astype(BF16)
 
-        loop(6, attend_back)
-        if r == 0:
-            step("output")
-        elif r == 1:
-            step("inner1")
-        else:
-            step("outer0", "outer1", "output")
+        span_loop(first, last, attend_back)
 
     def own_inputs(m):
         return jnp.concatenate(
@@ -610,53 +634,55 @@
     def all_inputs(m):
         return jnp.concatenate([x_all[r, :, pl.ds(384 * m, 384)] for r in range(3)], 0)
 
-    square_grads("query", own_inputs, q_own[...])
-    square_grads("key", all_inputs, wi[pl.ds(0, 1536)])
-    step("inner0", "query")
-    square_grads("value", all_inputs, wi[pl.ds(1536, 1536)])
-    step("outer0", "outer1", "inner1", "key")
-    put_sum(1, fold(q_own[...].astype(F32)))
+    def do_query_grads():
+        square_grads("query", own_inputs, q_own[...])
+
+    def do_key_grads():
+        square_grads("key", all_inputs, wi[pl.ds(0, 1536)])
+
+    def do_value_grads():
+        square_grads("value", all_inputs, wi[pl.ds(1536, 1536)])
 
     def value_sum(i, acc):
         return acc + fold(wi[pl.ds(pl.multiple_of(1536 + i * 128, 128), 128)].astype(F32))
 
-    put_sum(2, lax.fori_loop(0, 12, value_sum, nothing))
     mask_sums[...] = jnp.zeros((3, 8, 256), F32)
-    for r in range(3):
-
-        def d_in_part(n, carry):
+
+    def d_in_copy(kind, r):
+        if kind == 0:
+            source = wf.at[aligned(2 * r + 1 - core, 256)]
+            target, name = d_in0.at[r], "core"
+        else:
+            source = wf.at[aligned(4 * r + 2 * core + 1 - y, 128)]
+            target, name = d_in1.at[r], "y"
+        return pltpu.make_async_remote_copy(
+            src_ref=source,
+            dst_ref=target,
+            send_sem=x_send.at[3 + kind, r],
+            recv_sem=x_recv.at[3 + kind, r],
+            device_id=peer[name],
+            device_id_type=MESH,
+        )
+
+    def do_d_in(r):
+        def d_in_part(n):
             cols = aligned(n, 256)
             part = mm_t(wi[pl.ds(512 * r, 512)], wk[cols]) + mm_t(
                 wi[pl.ds(1536 + 512 * r, 512)], wv[cols]
             )
             for s in range(4):
-                piece = part[128 * s : 128 * s + 128]
-                wf[pl.ds(s * 384 + r * 128, 128), cols] = piece.astype(BF16)
+                block = 4 * r + 2 * (s % 2) + s // 2
+                wf[pl.ds(128 * block, 128), cols] = part[128 * s : 128 * s + 128].astype(BF16)
             mask_sums[n] = mask_sums[n] + fold(part * wide[:, r : r + 1])
-            return carry
-
-        lax.fori_loop(0, 3, d_in_part, 0)
-        if r == 0:
-            step("value")
-        elif r == 1:
-            step("output")
-
-    def d_in_copy(i):
-        if i < 2:
-            piece, target, name = 2 * i + 1 - core, d_in0.at[i], "core"
-        else:
-            piece, target, name = across, d_in1, "y"
-        return pltpu.make_async_remote_copy(
-            src_ref=wf.at[aligned(piece, 384)],
-            dst_ref=target,
-            send_sem=x_send.at[3, i],
-            recv_sem=x_recv.at[3, i],
-            device_id=peer[name],
-            device_id_type=MESH,
-        )
-
-    d_in_copy(0).start()
-    d_in_copy(1).start()
+
+        loop(3, d_in_part)
+        d_in_copy(0, r).start()
+
+    def d_in_pass(r):
+        d_in_copy(0, r).wait()
+        rows = aligned(4 * r + 2 * core + 1 - y, 128)
+        wf[rows] = wf[rows] + d_in0[r, aligned(1 - y, 128)]
+        d_in_copy(1, r).start()
 
     def own_part(i, acc):
         rows = aligned(i, 128)
@@ -666,45 +692,62 @@
         chosen = jnp.where(i == 0, chosen[:, 0:1], jnp.where(i == 1, chosen[:, 1:2], chosen[:, 2:3]))
         return acc + fold(part * chosen)
 
-    mask_sum = jnp.concatenate([mask_sums[n] for n in range(3)], axis=1)
-    put_sum(0, lax.fori_loop(0, 3, own_part, mask_sum))
-
-    def vector_copy(phase):
+    grad_copies = []
+
+    def d_in_close(r):
+        d_in_copy(1, r).wait()
+        rows = pl.ds(128 * r, 128)
+        value = (
+            d_res[rows]
+            + wf[aligned(4 * r + 2 * core + y, 128)].astype(F32)
+            + d_in0[r, aligned(y, 128)].astype(F32)
+            + d_in1[r].astype(F32)
+        )
+        chosen = wide[aligned(me, 128), r : r + 1] > 0.5
+        d_att[rows] = jnp.where(chosen, 0.0, value).astype(BF16)
+        copy = pltpu.make_async_copy(d_att.at[rows], grad_input.at[rows], local.at[18 + r])
+        copy.start()
+        grad_copies.append(copy)
+
+    axes = ("core", "x", "y", "zlo", "zhi")
+
+    def vector_copy(group, phase):
+        sums, came = (vec, vec_came) if group == 0 else (late, late_came)
         return pltpu.make_async_remote_copy(
-            src_ref=vec.at[phase],
-            dst_ref=vec_came.at[phase],
-            send_sem=v_send.at[phase],
-            recv_sem=v_recv.at[phase],
-            device_id=peer[names[phase]],
+            src_ref=sums.at[phase],
+            dst_ref=came.at[phase],
+            send_sem=v_send.at[group, phase],
+            recv_sem=v_recv.at[group, phase],
+            device_id=peer[axes[phase]],
             device_id_type=MESH,
         )
 
-    def vector_step(phase):
-        vector_copy(phase).wait()
-        vec[phase + 1] = vec[phase] + vec_came[phase]
+    def vector_step(group, phase):
+        vector_copy(group, phase).wait()
+        sums, came = (vec, vec_came) if group == 0 else (late, late_came)
+        sums[phase + 1] = sums[phase] + came[phase]
         if phase < 4:
-            vector_copy(phase + 1).start()
-
-    vector_copy(0).start()
-    d_in_copy(0).wait()
-    d_in_copy(1).wait()
-
-    def add_across(i):
-        rows = pl.ds(pl.multiple_of(across * 384 + i * 128, 128), 128)
-        wf[rows] = wf[rows] + d_in0[1 - y, aligned(i, 128)]
-
-    loop(3, add_across)
-    d_in_copy(2).start()
-    step("inner0")
-    vector_step(0)
-    step("query", "key")
-    vector_step(1)
+            vector_copy(group, phase + 1).start()
+
+    def do_late_sums():
+        late[0] = jnp.zeros((8, 768), F32)
+        mask_sum = jnp.concatenate([mask_sums[n] for n in range(3)], axis=1)
+        all_sums = (
+            lax.fori_loop(0, 3, own_part, mask_sum),
+            fold(q_own[...].astype(F32)),
+            lax.fori_loop(0, 12, value_sum, nothing),
+        )
+        for i, value in enumerate(all_sums):
+            late[0, i : i + 1] = jnp.sum(value, 0, keepdims=True)
+        vector_copy(1, 0).start()
+
     mine = (y, spot["zhi"], spot["zlo"], spot["x"])
 
-    def swap_copy(u):
+    def swap_copy(name):
+        u = STARTS.index(name)
         return pltpu.make_async_remote_copy(
-            src_ref=units[NAMES[u]].own.at[mine],
-            dst_ref=big5.at[u] if u < 2 else small5.at[u - 4],
+            src_ref=units[name].own.at[mine],
+            dst_ref=in5.at[u],
             send_sem=sends.at[u, 5],
             recv_sem=recvs.at[u, 5],
             device_id=peer["core"],
@@ -712,78 +755,82 @@
         )
 
     def close(name):
-        u, unit = NAMES.index(name), units[name]
+        unit = units[name]
         unit.copy(4).wait()
         result = unit.own[mine].astype(F32) + unit.inbox[4][...].astype(F32)
-        if u == 2 or u == 3:
-            out_inner[:, pl.ds(384 * (u - 2), 384)] = result
+        if name.startswith("inner"):
+            i = int(name[5:])
+            out_inner[pl.ds(48 * (i % 2), 48), pl.ds(384 * (i // 2), 384)] = result
             return
         unit.own[mine] = result.astype(BF16)
-        swap_copy(u).start()
-        put_half(u, core, result)
-
-    def put_half(u, side, value):
+        swap_copy(name).start()
+        put_half(name, core, result)
+
+    def put_half(name, side, value):
         value = jnp.where(core == 0, value[:, :192], pltpu.roll(value, 192, 1)[:, :192])
-        if u < 2:
-            out_outer[pl.ds(pl.multiple_of(side * 192 + u * 96, 96), 96)] = value
+        if name.startswith("outer"):
+            rows = side * 192 + int(name[5:]) * 48
+            out_outer[pl.ds(pl.multiple_of(rows, 48), 48)] = value
         else:
-            target = (out_output, out_query, out_key, out_value)[u - 4]
+            target = {
+                "output": out_output, "query": out_query, "key": out_key, "value": out_value
+            }[name]
             target[pl.ds(pl.multiple_of(side * 48, 48), 48)] = value
 
     def open_half(name):
-        u = NAMES.index(name)
-        swap_copy(u).wait()
-        put_half(u, 1 - core, (big5[u] if u < 2 else small5[u - 4]).astype(F32))
-
-    close("outer0")
-    close("outer1")
-    step("output", "value")
-    vector_step(2)
-    step("query", "key")
-    vector_step(3)
-    step("inner0", "inner1")
-    open_half("outer0")
-    open_half("outer1")
-    close("output")
-    step("value", "query", "key")
-    vector_step(4)
-    open_half("output")
-    close("inner0")
-    close("inner1")
-
-    d_in_copy(2).wait()
-
-    def finish_input(i):
-        rows = aligned(i, 128)
-        mine = pl.ds(pl.multiple_of(me * 384 + i * 128, 128), 128)
-        value = (
-            d_res[rows]
-            + wf[mine].astype(F32)
-            + d_in0[y, rows].astype(F32)
-            + d_in1[rows].astype(F32)
-        )
-        chosen = wide[aligned(me, 128)]
-        chosen = jnp.where(i == 0, chosen[:, 0:1], jnp.where(i == 1, chosen[:, 1:2], chosen[:, 2:3]))
-        d_att[rows] = jnp.where(chosen > 0.5, 0.0, value).astype(BF16)
-
-    loop(3, finish_input)
-    grad_copy = pltpu.make_async_copy(d_att, grad_input, local.at[18])
-    grad_copy.start()
+        swap_copy(name).wait()
+        put_half(name, 1 - core, in5[STARTS.index(name)].astype(F32))
+
+    stages = {
+        "d_hidden": lambda: loop(12, d_hidden_units),
+        "inner": do_inner_grads,
+        "d_first": do_d_first,
+        "fnb": do_first_norm_back,
+        "V1": lambda: vector_copy(0, 0).start(),
+        "dWo": do_output_grads,
+        "refill": refill_probs,
+        "dmixed": lambda: loop(3, d_mixed_part),
+        "dWq": do_query_grads,
+        "dWk": do_key_grads,
+        "dWv": do_value_grads,
+        "vec": do_late_sums,
+    }
+    for r in range(3):
+        stages[f"ab{r}0"] = lambda r=r: do_attend_back(r, 0, 3)
+        stages[f"ab{r}1"] = lambda r=r: do_attend_back(r, 3, 6)
+        stages[f"din{r}"] = lambda r=r: do_d_in(r)
+    count = {}
+    for name in PLAN:
+        if name in stages:
+            stages[name]()
+            continue
+        turn = count[name] = count.get(name, -1) + 1
+        if name in units:
+            if turn < 4:
+                units[name].step()
+                if turn == 0 and STARTS.index(name) < SLOTS:
+                    free_slot()
+            elif turn == 4:
+                close(name)
+            else:
+                open_half(name)
+        elif name in ("W1", "W2"):
+            vector_step(int(name[1]) - 1, turn)
+        elif name.startswith("dc"):
+            d_in_pass(int(name[2]))
+        else:
+            d_in_close(int(name[2]))
     out_vectors[...] = vec[5]
-    step("value")
-    close("query")
-    close("key")
-    close("value")
-    open_half("query")
-    open_half("key")
-    open_half("value")
-    grad_copy.wait()
+    out_vectors[0:3] = late[5, 0:3]
+    for copy in grad_copies:
+        copy.wait()
 
 
 def hand_out(*refs):
     sources, vectors, targets, rows = refs[:8], refs[8], refs[9:17], refs[17:27]
-    for source, target in zip(sources, targets):
+    for source, target in zip(sources[:7], targets[:7]):
         target[...] = source[...]
+    targets[7][...] = sources[7][...].T
     for i, place in enumerate((0, 1, 2, 3, 4, 5, None, 10, 11, 12)):
         if place is not None:
             rows[i][...] = vectors[place]
@@ -862,32 +909,28 @@
             fl(512, 8),
             fl(12, 8, 256),
             fl(3, 8, 256),
-            bf(4, 2, 2, 2, 2, 2, 96, 384),
-            bf(4, 2, 2, 2, 2, 2, 48, 384),
-            bf(SLOTS, 2, 2, 2, 2, 96, 384),
-            bf(4, 2, 2, 2, 96, 384),
-            bf(4, 2, 2, 96, 384),
-            bf(4, 2, 96, 384),
-            bf(4, 96, 384),
-            bf(2, 96, 384),
-            bf(4, 2, 2, 2, 48, 384),
-            bf(4, 2, 2, 48, 384),
-            bf(4, 2, 48, 384),
-            bf(4, 48, 384),
-            bf(4, 48, 384),
-            bf(2, 384, 768),
-            bf(384, 768),
+            bf(12, 2, 2, 2, 2, 2, 48, 384),
+            bf(SLOTS, 2, 2, 2, 2, 48, 384),
+            bf(12, 2, 2, 2, 48, 384),
+            bf(12, 2, 2, 48, 384),
+            bf(12, 2, 48, 384),
+            bf(12, 48, 384),
+            bf(12, 48, 384),
+            bf(3, 256, 768),
+            bf(3, 128, 768),
             fl(6, 16, 768),
             fl(5, 16, 768),
-            dma(8, 6),
-            dma(8, 6),
-            dma(4, 3),
-            dma(4, 3),
+            fl(6, 8, 768),
+            fl(5, 8, 768),
+            dma(12, 6),
+            dma(12, 6),
+            dma(5, 3),
+            dma(5, 3),
             dma(3),
             dma(3),
-            dma(5),
-            dma(5),
-            dma(19),
+            dma(2, 5),
+            dma(2, 5),
+            dma(21),
             pltpu.SemaphoreType.REGULAR,
         ],
         compiler_params=pltpu.CompilerParams(
@@ -921,7 +964,8 @@
     wide_row = shape((768,), F32)
     handed = pl.pallas_call(
         hand_out,
-        out_shape=[shape(v.shape, v.dtype) for v in arrays]
+        out_shape=[shape(v.shape, v.dtype) for v in arrays[:7]]
+        + [shape((192, 384), F32)]
         + [wide_row] * 6
         + [shape((3072,), F32)]
         + [wide_row] * 3,
@@ -946,7 +990,7 @@
         g_shift,
         g_inner,
         g_inner_bias,
-        g_outer,
+        g_outer.T,
         *g_last,
     )
 

time: 150 us -> 124 us (0.83)
  Pallas kernels: 147 us -> 123 us
  local copies, waits for them, and re-layouts: 1.86 us -> 0 us
    pallas_call x1, Pallas kernels: 144 us -> 120 us  [fused_layer(): pl.pallas_call(layer_body, out_shape=[shape((384, 768), BF16), shape((384...]
    unnamed x1 -> x0, local copies, waits for them, and re-layouts: 1.86 us -> none
where the time goes in v4:
time: 124 us; the launch traced here: 123 us
  Pallas kernels  123 us (99%)
    pallas_call x1, Pallas kernels, fused_layer(): pl.pallas_call(layer_body, out_shape=[shape((384, 768), BF16), shape((384...  120 us
    pallas_call x1, Pallas kernels, fused_layer(): pl.pallas_call(hand_out, out_shape=[shape(v.shape, v.dtype) for v in arra...  3.04 us

profile of v4, /device:TPU:0, one launch (start us, length us, event | category | flops | bytes accessed | tf_op | source)
XLA Modules:
  0.0 123.4 jit_solution(7712409432577542414)
XLA Ops:
  0.7 119.5 %fused_layer.1 = (bf16[384,768]{1,0:T(8,128)(2,1)}, bf16[384,768]{1,0:T(8,128)(2,1)}, bf16[9216,256]{1,0:T(8,128)(2,1)}, f32[96,192]{1,0:T(8,128)}, f32[96,192]{...) custom-call(bf16[3,128,768]{2,1,0:T(8,128)(2,1)} %hidden.1, ...), custom_call_target="tpu_custom_call" | custom-call | tf_op jit(solution)/shard_map/fused_layer/pallas_call | solution.py:871
  120.2 3.0 %hand_out.1 = (bf16[384,768]{1,0:T(8,128)(2,1)}, bf16[384,768]{1,0:T(8,128)(2,1)}, f32[96,192]{1,0:T(8,128)}, f32[96,192]{1,0:T(8,128)}, f32[96,192]{1,0:T(8,128...) custom-call(bf16[384,768]{1,0:T(8,128)(2,1)} %get-tuple-element.45.r, ...), custom_call_target="tpu_custom_call" | custom-call | tf_op jit(solution)/shard_map/hand_out/pallas_call | solution.py:965
